TPU v7x, 256 devices: a whole 4x4x8 slice. The times are simulated.
256 devices in a mesh: date: 32 (over y_hi, z, core), strip: 8 (over x, y_lo).
Axes of the slice: x: 4, y: 4 (y_hi: 2, y_lo: 2; y = y_hi * 2 + y_lo), z: 8, core: 2. Of those that a mesh axis runs over, the one named last changes fastest.
Arguments:
- slc: bfloat16 [64, 2, 320, 2560], P('date', None, 'strip')
- pair_second: int32 [64, 6], P('date'), may hold values from 0 to 63, as said below
- pair_count: int32 [64], P('date'), may hold values from 0 to 6, as said below
Outputs:
- interferogram: float32 [64, 6, 2, 64, 128], P('date', None, None, 'strip')
- coherence: float32 [64, 6, 64, 128], P('date', None, 'strip')
Inputs may be any that keep to these rules, and one draw needn't show every extreme that they name: `pair_count`: date d has min(6, 63 - d, a drawn count of 2 to 6) pairs; date 0 has 6. For s < pair_count[d], pair_second[d, s] lies in d + 1 to d + 8, distinct within a date; the other slots hold d.
All inputs are finite; a program needn't handle non-finite values.
Results may differ from a plain program's by a relative error of at most 0.0003.
Values may be sent and summed in bfloat16 or wider, within the bound.
A program may use at most 64 MiB of HBM per device.

v0:
```python
import jax
import jax.numpy as jnp
from jax import lax
from jax.sharding import PartitionSpec as P

LOOK_AZ = 5
LOOK_RG = 20
WIN = 7
SLOTS = 6
HOPS = 4


def shifted(block, axis, distance):
    devices = range(lax.axis_size(axis))
    route = [(i - distance, i) for i in devices if i - distance in devices]
    return lax.ppermute(block, axis, route)


def padded_2(cells, sides, width):
    for axis, dim in sides:
        count = lax.axis_size(axis)
        ends = count - 1
        head = lax.slice_in_dim(cells, 0, width, axis=dim)
        tail = lax.slice_in_dim(cells, cells.shape[dim] - width, cells.shape[dim], axis=dim)
        cells = jnp.concatenate(
            [
                lax.ppermute(tail, axis, [(i, (i + 1) % count) for i in range(ends)]),
                cells,
                lax.ppermute(head, axis, [((i + 1) % count, i) for i in range(ends)]),
            ],
            axis=dim,
        )
    return cells


def box_sum(field, rows):
    half = WIN // 2
    cols = field.shape[-1]
    across = field[..., 0:rows, :]
    for shift_rows in range(1, WIN):
        across = across + field[..., shift_rows : shift_rows + rows, :]
    widths = [(0, 0)] * (field.ndim - 1) + [(half, half)]
    padded = jnp.pad(across, widths)
    total = padded[..., 0:cols]
    for shift_cols in range(1, WIN):
        total = total + padded[..., shift_cols : shift_cols + cols]
    return total


def multilook(field, width):
    range_looks = width // LOOK_RG
    az_looks = field.shape[-2] // LOOK_AZ
    table = (jnp.arange(width)[:, None] // LOOK_RG == jnp.arange(range_looks)[None, :]).astype(
        jnp.float32
    )
    flat = jnp.dot(field.reshape(-1, width), table, precision=lax.Precision.HIGHEST)
    back = flat.reshape(field.shape[:-2] + (az_looks, LOOK_AZ, range_looks))
    return jnp.sum(back, axis=-2) / (LOOK_AZ * LOOK_RG)


def slot_terms(own, pool, seconds, start_date):
    width = own.shape[-1]
    count_dates = own.shape[0]
    az_looks = own.shape[-2] // LOOK_AZ
    range_looks = width // LOOK_RG
    pool_size = pool.shape[0]

    def pair_terms(slot):
        wanted = lax.dynamic_index_in_dim(seconds, slot, 1, False) - start_date
        wanted = jnp.clip(wanted, 0, pool_size - 1)
        partner = jnp.take(pool, wanted, axis=0).astype(jnp.float32)
        prod_real = own[:, 0] * partner[:, 0] + own[:, 1] * partner[:, 1]
        prod_imag = own[:, 1] * partner[:, 0] - own[:, 0] * partner[:, 1]
        power_sec = partner[:, 0] * partner[:, 0] + partner[:, 1] * partner[:, 1]
        return multilook(jnp.stack([prod_real, prod_imag, power_sec], 1), width)

    terms = jnp.stack([pair_terms(slot) for slot in range(SLOTS)], 1)
    look_ref = multilook(own[:, 0] * own[:, 0] + own[:, 1] * own[:, 1], width)
    ref_grid = jnp.broadcast_to(
        look_ref[:, None, None], (count_dates, SLOTS, 1, az_looks, range_looks)
    )
    return (terms, jnp.concatenate([terms, ref_grid], 2))


def shards(slc, pair_second, pair_count):
    dates_here = slc.shape[0]
    az_rows = slc.shape[2]
    az_looks = az_rows // LOOK_AZ
    first_date = lax.axis_index("date") * dates_here
    blocks = [slc]
    latest = slc
    for hop in range(1, HOPS + 1):
        latest = shifted(slc, "date", -hop)
        blocks.append(latest)
    pool = jnp.concatenate(blocks, 0)
    own = slc.astype(jnp.float32)
    terms, grids = slot_terms(own, pool, pair_second, first_date)
    padded = padded_2(grids, (("strip", 3),), WIN // 2)
    boxes = box_sum(padded, az_looks)
    coher = jnp.sqrt(boxes[:, :, 0] * boxes[:, :, 0] + boxes[:, :, 1] * boxes[:, :, 1]) / jnp.sqrt(
        boxes[:, :, 3] * boxes[:, :, 2]
    )
    used = jnp.arange(SLOTS)[None, :] < pair_count[:, None]
    interferogram = jnp.where(used[:, :, None, None, None], terms[:, :, 0:2], jnp.float32(0.0))
    coherence = jnp.where(used[:, :, None, None], coher, jnp.float32(0.0))
    return (interferogram, coherence)


def solution(mesh):
    in_specs = (P("date", None, "strip", None), P("date", None), P("date"))
    out_specs = (P("date", None, None, "strip", None), P("date", None, "strip", None))
    return jax.shard_map(shards, mesh=mesh, in_specs=in_specs, out_specs=out_specs, check_vma=False)
```

profile of v0, /device:TPU:200, one launch (start us, length us, event | category | flops | bytes accessed | tf_op | source)
XLA Modules:
  0.0 159.4 jit_solution(3314215661574596507)
XLA Ops:
  0.6 2.5 %collective-permute-start = (bf16[2,2,40,2560]{3,2,1,0:T(8,128)(2,1)}, bf16[2,2,40,2560]{3,2,1,0:T(8,128)(2,1)}, u32[]{:S(2)}, u32[]{:S(2)}) collective-permute-start(bf16[2,2,40,2560]{3,2,1,0:T(8,128)(2,1)} %param.5), channel_id=1, source_target_pairs={{8,0},{16,8},{24,16},{32,24},{40,32},{48,40},{56,48},{64,56},{72,6... | collective-permute-start | bytes 2457608 | tf_op jit(solution)/shard_map/ppermute | solution.py:16
  3.1 2.9 %collective-permute-start.1 = (bf16[2,2,40,2560]{3,2,1,0:T(8,128)(2,1)}, bf16[2,2,40,2560]{3,2,1,0:T(8,128)(2,1)}, u32[]{:S(2)}, u32[]{:S(2)}) collective-permute-start(bf16[2,2,40,2560]{3,2,1,0:T(8,128)(2,1)} %param.5), channel_id=1, source_target_pairs={{16,0},{24,8},{32,16},{40,24},{48,32},{56,40},{64,48},{72,56},{80,... | collective-permute-start | bytes 2457608 | tf_op jit(solution)/shard_map/ppermute | solution.py:16
  6.1 2.0 %collective-permute-start.2 = (bf16[2,2,40,2560]{3,2,1,0:T(8,128)(2,1)}, bf16[2,2,40,2560]{3,2,1,0:T(8,128)(2,1)S(1)}, u32[]{:S(2)}, u32[]{:S(2)}) collective-permute-start(bf16[2,2,40,2560]{3,2,1,0:T(8,128)(2,1)} %param.5), channel_id=1, source_target_pairs={{24,0},{32,8},{40,16},{48,24},{56,32},{64,40},{72,48},{80,56},{88,... | collective-permute-start | bytes 2457608 | tf_op jit(solution)/shard_map/ppermute | solution.py:16
  8.1 1.9 %collective-permute-start.3 = (bf16[2,2,40,2560]{3,2,1,0:T(8,128)(2,1)}, bf16[2,2,40,2560]{3,2,1,0:T(8,128)(2,1)S(1)}, u32[]{:S(2)}, u32[]{:S(2)}) collective-permute-start(bf16[2,2,40,2560]{3,2,1,0:T(8,128)(2,1)} %param.5), channel_id=1, source_target_pairs={{32,0},{40,8},{48,16},{56,24},{64,32},{72,40},{80,48},{88,56},{96,... | collective-permute-start | bytes 2457608 | tf_op jit(solution)/shard_map/ppermute | solution.py:16
  10.0 2.5 %fusion.84 = (f32[2,2,40,2560]{3,2,1,0:T(8,128)S(1)}, bf16[10,2,40,2560]{3,2,1,0:T(8,128)(2,1)}) fusion(bf16[2,2,40,2560]{3,2,1,0:T(8,128)(2,1)} %param.5), kind=kLoop, calls=%fused_computation.149 | loop fusion | flops 409599 | bytes 3276800 | tf_op jit(solution)/shard_map/convert_element_type | solution.py:96
  13.1 6.9 %collective-permute-done = bf16[2,2,40,2560]{3,2,1,0:T(8,128)(2,1)} collective-permute-done((bf16[2,2,40,2560]{3,2,1,0:T(8,128)(2,1)}, bf16[2,2,40,2560]{3,2,1,0:T(8,128)(2,1)}, u32[]{:S(2)}, u32[]{:S(2)}) %collective-permute-start) | collective-permute-done | bytes 819232 | tf_op jit(solution)/shard_map/ppermute | solution.py:16
  20.0 2.1 %constant_dynamic-update-slice_fusion.3 = bf16[10,2,40,2560]{3,2,1,0:T(8,128)(2,1)} fusion(bf16[10,2,40,2560]{3,2,1,0:T(8,128)(2,1)} %get-tuple-element.37, bf16[2,2,40,2560]{3,2,1,0:T(8,128)(2,1)} %collective-permute-done), kind=kLoop, calls=%fused_computation.117 | loop fusion | bytes 1638400
  22.1 16.9 %collective-permute-done.1 = bf16[2,2,40,2560]{3,2,1,0:T(8,128)(2,1)} collective-permute-done((bf16[2,2,40,2560]{3,2,1,0:T(8,128)(2,1)}, bf16[2,2,40,2560]{3,2,1,0:T(8,128)(2,1)}, u32[]{:S(2)}, u32[]{:S(2)}) %collective-permute-start.1) | collective-permute-done | bytes 819232 | tf_op jit(solution)/shard_map/ppermute | solution.py:16
  39.0 2.1 %constant_dynamic-update-slice_fusion.2 = bf16[10,2,40,2560]{3,2,1,0:T(8,128)(2,1)} fusion(bf16[10,2,40,2560]{3,2,1,0:T(8,128)(2,1)} %constant_dynamic-update-slice_fusion.3, bf16[2,2,40,2560]{3,2,1,0:T(8,128)(2,1)} %collective-permute-done.1), kind=kLoop, calls=%fused_computation.116 | loop fusion | bytes 1638400
  41.1 40.3 %collective-permute-done.2 = bf16[2,2,40,2560]{3,2,1,0:T(8,128)(2,1)S(1)} collective-permute-done((bf16[2,2,40,2560]{3,2,1,0:T(8,128)(2,1)}, bf16[2,2,40,2560]{3,2,1,0:T(8,128)(2,1)S(1)}, u32[]{:S(2)}, u32[]{:S(2)}) %collective-permute-start.2) | collective-permute-done | bytes 819232 | tf_op jit(solution)/shard_map/ppermute | solution.py:16
  82.4 15.3 %collective-permute-done.3 = bf16[2,2,40,2560]{3,2,1,0:T(8,128)(2,1)S(1)} collective-permute-done((bf16[2,2,40,2560]{3,2,1,0:T(8,128)(2,1)}, bf16[2,2,40,2560]{3,2,1,0:T(8,128)(2,1)S(1)}, u32[]{:S(2)}, u32[]{:S(2)}) %collective-permute-start.3) | collective-permute-done | bytes 819232 | tf_op jit(solution)/shard_map/ppermute | solution.py:16
  98.7 2.8 %gather_fusion = bf16[2,2,40,2560]{3,2,1,0:T(8,128)(2,1)S(1)} fusion(bf16[10,2,40,2560]{3,2,1,0:T(8,128)(2,1)} %constant_dynamic-update-slice_fusion, s32[1024]{0:T(1024)S(1)} %pad_clamp_fusion.5), kind=kCustom, calls=%fused_computation.clone | custom fusion | bytes 1638408 | tf_op jit(solution)/shard_map/jit(_take)/gather | solution.py:71
  102.2 1.9 %copy.32 = f32[2,3,40,2560]{3,0,2,1:T(2,128)S(1)} copy(f32[2,3,40,2560]{3,2,1,0:T(8,128)S(1)} %pad_maximum_fusion) | data formatting | bytes 4915200 | tf_op jit(solution)/shard_map/stack | solution.py:75
  104.1 1.6 fusion.22
  105.7 2.8 %gather_fusion.1 = bf16[2,2,40,2560]{3,2,1,0:T(8,128)(2,1)S(1)} fusion(bf16[10,2,40,2560]{3,2,1,0:T(8,128)(2,1)} %constant_dynamic-update-slice_fusion, s32[1024]{0:T(1024)S(1)} %pad_clamp_fusion.4), kind=kCustom, calls=%fused_computation.1.clone | custom fusion | bytes 1638408 | tf_op jit(solution)/shard_map/jit(_take)/gather | solution.py:71
  110.0 1.9 %copy.34 = f32[2,3,40,2560]{3,0,2,1:T(2,128)S(1)} copy(f32[2,3,40,2560]{3,2,1,0:T(8,128)S(1)} %pad_maximum_fusion.1) | data formatting | bytes 4915200 | tf_op jit(solution)/shard_map/stack | solution.py:75
  112.0 1.6 fusion.27
  113.5 2.8 %gather_fusion.5 = bf16[2,2,40,2560]{3,2,1,0:T(8,128)(2,1)S(1)} fusion(bf16[10,2,40,2560]{3,2,1,0:T(8,128)(2,1)} %constant_dynamic-update-slice_fusion, s32[1024]{0:T(1024)S(1)} %pad_clamp_fusion), kind=kCustom, calls=%fused_computation.5.clone | custom fusion | bytes 1638408 | tf_op jit(solution)/shard_map/jit(_take)/gather | solution.py:71
  116.3 2.8 %gather_fusion.2 = bf16[2,2,40,2560]{3,2,1,0:T(8,128)(2,1)S(1)} fusion(bf16[10,2,40,2560]{3,2,1,0:T(8,128)(2,1)} %constant_dynamic-update-slice_fusion, s32[1024]{0:T(1024)S(1)} %pad_clamp_fusion.3), kind=kCustom, calls=%fused_computation.2.clone | custom fusion | bytes 1638408 | tf_op jit(solution)/shard_map/jit(_take)/gather | solution.py:71
  121.3 2.1 %copy.36 = f32[2,3,40,2560]{3,0,2,1:T(2,128)S(1)} copy(f32[2,3,40,2560]{3,2,1,0:T(8,128)S(1)} %pad_maximum_fusion.2) | data formatting | bytes 4915200 | tf_op jit(solution)/shard_map/stack | solution.py:75
  123.4 1.6 fusion.32
  124.9 3.7 %gather_fusion.4 = bf16[2,2,40,2560]{3,2,1,0:T(8,128)(2,1)} fusion(bf16[10,2,40,2560]{3,2,1,0:T(8,128)(2,1)} %constant_dynamic-update-slice_fusion, s32[1024]{0:T(1024)S(1)} %pad_clamp_fusion.1), kind=kCustom, calls=%fused_computation.4.clone | custom fusion | bytes 1638408 | tf_op jit(solution)/shard_map/jit(_take)/gather | solution.py:71
  128.6 3.7 %gather_fusion.3 = bf16[2,2,40,2560]{3,2,1,0:T(8,128)(2,1)} fusion(bf16[10,2,40,2560]{3,2,1,0:T(8,128)(2,1)} %constant_dynamic-update-slice_fusion, s32[1024]{0:T(1024)S(1)} %pad_clamp_fusion.2), kind=kCustom, calls=%fused_computation.3.clone | custom fusion | bytes 1638408 | tf_op jit(solution)/shard_map/jit(_take)/gather | solution.py:71
  134.7 1.9 %copy.38 = f32[2,3,40,2560]{3,0,2,1:T(2,128)S(1)} copy(f32[2,3,40,2560]{3,2,1,0:T(8,128)S(1)} %pad_maximum_fusion.3) | data formatting | bytes 4915200 | tf_op jit(solution)/shard_map/stack | solution.py:75
  136.6 1.6 fusion.37
  138.4 1.9 %copy.40 = f32[2,3,40,2560]{3,0,2,1:T(2,128)S(1)} copy(f32[2,3,40,2560]{3,2,1,0:T(8,128)S(1)} %pad_maximum_fusion.4) | data formatting | bytes 4915200 | tf_op jit(solution)/shard_map/stack | solution.py:75
  140.3 1.6 fusion.42
  142.1 2.1 %copy.42 = f32[2,3,40,2560]{3,0,2,1:T(2,128)S(1)} copy(f32[2,3,40,2560]{3,2,1,0:T(8,128)S(1)} %pad_maximum_fusion.5) | data formatting | bytes 4915200 | tf_op jit(solution)/shard_map/stack | solution.py:75
  144.2 1.6 fusion.47
  147.4 3.3 %collective-permute-start.4 = (f32[2,6,4,3,128]{4,3,2,0,1:T(4,128)S(1)}, f32[2,6,4,3,128]{4,3,2,0,1:T(4,128)S(1)}, u32[]{:S(2)}, u32[]{:S(2)}) collective-permute-start(f32[2,6,4,3,128]{4,3,2,0,1:T(4,128)S(1)} %get-tuple-element.40), channel_id=1, source_target_pairs={{0,1},{1,2},{2,3},{3,4},{4,5},{5,6},{6,7},{8,9},{9,10},{10,11},{11... | collective-permute-start | bytes 221192 | tf_op jit(solution)/shard_map/ppermute | solution.py:27
  150.7 2.6 %collective-permute-start.5 = (f32[2,6,4,3,128]{4,3,2,0,1:T(4,128)S(1)}, f32[2,6,4,3,128]{4,3,2,0,1:T(4,128)S(1)}, u32[]{:S(2)}, u32[]{:S(2)}) collective-permute-start(f32[2,6,4,3,128]{4,3,2,0,1:T(4,128)S(1)} %get-tuple-element.41), channel_id=1, source_target_pairs={{1,0},{2,1},{3,2},{4,3},{5,4},{6,5},{7,6},{9,8},{10,9},{11,10},{12... | collective-permute-start | bytes 221192 | tf_op jit(solution)/shard_map/ppermute | solution.py:29
  154.0 4.1 %collective-permute-done.5 = f32[2,6,4,3,128]{4,3,2,0,1:T(4,128)S(1)} collective-permute-done((f32[2,6,4,3,128]{4,3,2,0,1:T(4,128)S(1)}, f32[2,6,4,3,128]{4,3,2,0,1:T(4,128)S(1)}, u32[]{:S(2)}, u32[]{:S(2)}) %collective-permute-start.5) | collective-permute-done | bytes 73760 | tf_op jit(solution)/shard_map/ppermute | solution.py:29
  (64 shorter events, 13.1 us)
Async XLA Ops:
  0.6 12.0 %copy-start.3 = (s32[2,6]{1,0:T(2,128)S(1)}, s32[2,6]{1,0:T(2,128)}, u32[]{:S(2)}) copy-start(s32[2,6]{1,0:T(2,128)} %param.6) | copy-start | bytes 148
  0.6 12.3 %copy-start.4 = (s32[2]{0:T(128)S(1)}, s32[2]{0:T(128)}, u32[]{:S(2)}) copy-start(s32[2]{0:T(128)} %param.7) | copy-start | bytes 28
  0.6 19.3 %collective-permute-start = (bf16[2,2,40,2560]{3,2,1,0:T(8,128)(2,1)}, bf16[2,2,40,2560]{3,2,1,0:T(8,128)(2,1)}, u32[]{:S(2)}, u32[]{:S(2)}) collective-permute-start(bf16[2,2,40,2560]{3,2,1,0:T(8,128)(2,1)} %param.5), channel_id=1, source_target_pairs={{8,0},{16,8},{24,16},{32,24},{40,32},{48,40},{56,48},{64,56},{72,6... | collective-permute-start | bytes 2457608 | tf_op jit(solution)/shard_map/ppermute | solution.py:16
  3.1 35.9 %collective-permute-start.1 = (bf16[2,2,40,2560]{3,2,1,0:T(8,128)(2,1)}, bf16[2,2,40,2560]{3,2,1,0:T(8,128)(2,1)}, u32[]{:S(2)}, u32[]{:S(2)}) collective-permute-start(bf16[2,2,40,2560]{3,2,1,0:T(8,128)(2,1)} %param.5), channel_id=1, source_target_pairs={{16,0},{24,8},{32,16},{40,24},{48,32},{56,40},{64,48},{72,56},{80,... | collective-permute-start | bytes 2457608 | tf_op jit(solution)/shard_map/ppermute | solution.py:16
  6.1 75.4 %collective-permute-start.2 = (bf16[2,2,40,2560]{3,2,1,0:T(8,128)(2,1)}, bf16[2,2,40,2560]{3,2,1,0:T(8,128)(2,1)S(1)}, u32[]{:S(2)}, u32[]{:S(2)}) collective-permute-start(bf16[2,2,40,2560]{3,2,1,0:T(8,128)(2,1)} %param.5), channel_id=1, source_target_pairs={{24,0},{32,8},{40,16},{48,24},{56,32},{64,40},{72,48},{80,56},{88,... | collective-permute-start | bytes 2457608 | tf_op jit(solution)/shard_map/ppermute | solution.py:16
  8.1 89.6 %collective-permute-start.3 = (bf16[2,2,40,2560]{3,2,1,0:T(8,128)(2,1)}, bf16[2,2,40,2560]{3,2,1,0:T(8,128)(2,1)S(1)}, u32[]{:S(2)}, u32[]{:S(2)}) collective-permute-start(bf16[2,2,40,2560]{3,2,1,0:T(8,128)(2,1)} %param.5), channel_id=1, source_target_pairs={{32,0},{40,8},{48,16},{56,24},{64,32},{72,40},{80,48},{88,56},{96,... | collective-permute-start | bytes 2457608 | tf_op jit(solution)/shard_map/ppermute | solution.py:16
  132.3 1.5 copy-start.2
  140.3 1.6 copy-start.1
  144.2 1.6 copy-start
  147.4 6.6 %collective-permute-start.4 = (f32[2,6,4,3,128]{4,3,2,0,1:T(4,128)S(1)}, f32[2,6,4,3,128]{4,3,2,0,1:T(4,128)S(1)}, u32[]{:S(2)}, u32[]{:S(2)}) collective-permute-start(f32[2,6,4,3,128]{4,3,2,0,1:T(4,128)S(1)} %get-tuple-element.40), channel_id=1, source_target_pairs={{0,1},{1,2},{2,3},{3,4},{4,5},{5,6},{6,7},{8,9},{9,10},{10,11},{11... | collective-permute-start | bytes 221192 | tf_op jit(solution)/shard_map/ppermute | solution.py:27
  150.7 7.4 %collective-permute-start.5 = (f32[2,6,4,3,128]{4,3,2,0,1:T(4,128)S(1)}, f32[2,6,4,3,128]{4,3,2,0,1:T(4,128)S(1)}, u32[]{:S(2)}, u32[]{:S(2)}) collective-permute-start(f32[2,6,4,3,128]{4,3,2,0,1:T(4,128)S(1)} %get-tuple-element.41), channel_id=1, source_target_pairs={{1,0},{2,1},{3,2},{4,3},{5,4},{6,5},{7,6},{9,8},{10,9},{11,10},{12... | collective-permute-start | bytes 221192 | tf_op jit(solution)/shard_map/ppermute | solution.py:29
where the time goes:
time: 160 us; the launch traced here: 159 us
  waiting for transfers between devices  83.6 us (52%)
  local copies, waits for them, and re-layouts  38.2 us (24%)
  starting transfers between devices  15.2 us (10%)
  other arithmetic  11 us (7%)
  matrix products  10.2 us (6%)
    ppermute x4, waiting for transfers between devices, shifted(): return lax.ppermute(block, axis, route)  79.5 us
    gather x6, local copies, waits for them, and re-layouts, pair_terms(): partner = jnp.take(pool, wanted, axis=0).astype(jnp.float32)  18.4 us
    another operation x6, local copies, waits for them, and re-layouts, pair_terms(): return multilook(jnp.stack([prod_real, prod_imag, power_sec], 1), width)  11.8 us
    dot_general x7, matrix products, multilook(): jnp.dot(field.reshape(-1, width), table, precision=lax.Precision.HIGHEST)  10.2 us
    ppermute x4, starting transfers between devices, shifted(): return lax.ppermute(block, axis, route)  9.36 us
    unnamed x15, local copies, waits for them, and re-layouts  6.45 us
    ppermute x1, waiting for transfers between devices, padded_2(): lax.ppermute(head, axis, [((i + 1) % count, i) for i in range(ends)])  4.1 us
    ppermute x1, starting transfers between devices, padded_2(): lax.ppermute(tail, axis, [(i, (i + 1) % count) for i in range(ends)])  3.29 us
  transfers between devices with their start and end apart: 6, of which 5 were waited for; matrix products, arithmetic and copies ran while one was open for 6% of the time, Pallas kernels for 0%

commit v1 on v0

v1 whole, which is shorter than its diff:
```python
import jax
import jax.numpy as jnp
from jax import lax
from jax.experimental import pallas as pl
from jax.experimental.pallas import tpu as pltpu
from jax.sharding import PartitionSpec as P

MESH = pl.DeviceIdType.MESH
F32 = jnp.float32
BF16 = jnp.bfloat16

LOOK_AZ = 5
LOOK_RG = 20
SLOTS = 6
OFFS = 8
CHIPS = 16
STRIPS = 8
ROWS = 40
WIDTH = 2560
HALF = WIDTH // 2
LOOKS = ROWS // LOOK_AZ
CELLS = 128
PLANE_SCALE = 1.0 / (LOOK_AZ * LOOK_RG)

SAME = [(0, 1), (0, 2), (0, 3), (1, 2), (1, 3), (2, 3)]


def pair(a, b):
    return ("pair", a, b)


def power(a, b):
    return ("power", a, b)


STAGES = [
    [pair((0, a), (0, b)) for a, b in SAME] + [power((0, 0), (0, 1)), power((0, 2), (0, 3))],
    [pair((0, a), (1, 0)) for a in range(4)],
    [pair((0, a), (1, 1)) for a in range(4)] + [power((1, 0), (1, 1))],
    [pair((0, a), (1, 2)) for a in range(4)],
    [pair((0, a), (1, 3)) for a in range(4)] + [power((1, 2), (1, 3))],
]
STARTS = [0, 8, 12, 17, 21]
N_OWN = 26
IA, IB = 16, 25
BACK = [
    [],
    [(pair((-1, 3), (1, 0)), 0)],
    [(pair((-1, 3), (1, 1)), 1), (pair((-1, 2), (1, 0)), 2), (pair((-1, 2), (1, 1)), 3)],
    [(pair((-1, 3), (1, 2)), 4), (pair((-1, 2), (1, 2)), 5), (pair((-1, 1), (1, 0)), 9), (pair((-1, 1), (1, 1)), 10)],
    [(pair((-1, 3), (1, 3)), 7), (pair((-1, 0), (1, 0)), 12)],
]
BACK_IA, BACK_IB = (6, 11), (8, 13)
N_BACK = 14
BACK_SENDS = [(2, 1, 0, 4, 0), (3, 0, 9, 3, 4), (3, 1, 4, 3, 4), (4, 0, 12, 2, 7), (4, 1, 7, 2, 7)]
N_PLANES = N_OWN + 9


def kernel(slc, second, count, ifg, coh, tiles, looks, sums, table, res, back, lsem, xs, xr, us, ur, vs, vr, ps, pr, bs, br):
    date = lax.axis_index("date")
    strip = lax.axis_index("strip")
    q = date // 2
    c = date % 2
    other = 1 - c
    has_prev, has_next = q > 0, q < CHIPS - 1
    has_up, has_down = strip > 0, strip < STRIPS - 1

    def device(dq, core, ds):
        return ((q + dq) * 2 + core, strip + ds)

    def side_ok(ds):
        return {0: None, -1: has_up, 1: has_down}[ds]

    def chip_ok(dq):
        return {0: None, -1: has_prev, 1: has_next}[dq]

    def when(*conditions):
        conditions = [x for x in conditions if x is not None]
        if not conditions:
            return lambda f: f()
        total = conditions[0]
        for x in conditions[1:]:
            total = jnp.logical_and(total, x)
        return pl.when(total)

    barrier = pltpu.get_barrier_semaphore()
    pl.semaphore_signal(barrier, inc=1, device_id=device(0, other, 0), device_id_type=MESH)
    for dq in (-1, 1, 0):
        for ds in (0, -1, 1):
            if (dq, ds) == (0, 0):
                continue

            @when(chip_ok(dq), side_ok(ds))
            def _():
                for core in range(2):
                    pl.semaphore_signal(barrier, inc=1, device_id=device(dq, core, ds), device_id_type=MESH)

    own_copy = pltpu.make_async_copy(
        slc.at[:, :, :, pl.ds(pl.multiple_of(c * HALF, HALF), HALF)], tiles.at[1, pl.ds(2 * c, 2)], lsem
    )
    own_copy.start()

    first = lax.broadcasted_iota(jnp.int32, (CELLS, CELLS), 1) * LOOK_RG
    lane = lax.broadcasted_iota(jnp.int32, (CELLS, CELLS), 0)

    def fill(i, carry):
        delta = lane + i * CELLS - first
        inside = jnp.logical_and(delta >= 0, delta < LOOK_RG)
        table[pl.ds(pl.multiple_of(i * CELLS, CELLS), CELLS), :] = jnp.where(inside, 1.0, 0.0).astype(BF16)
        return carry

    lax.fori_loop(0, WIDTH // CELLS, fill, 0)
    row = lax.broadcasted_iota(jnp.int32, (ROWS, ROWS), 0)
    col = lax.broadcasted_iota(jnp.int32, (ROWS, ROWS), 1)
    order = jnp.where(col == LOOK_AZ * (row % LOOKS) + row // LOOKS, 1.0, 0.0).astype(BF16)

    @pl.when(jnp.logical_not(has_up))
    def _():
        res[0] = jnp.zeros(res.shape[1:], F32)

    @pl.when(jnp.logical_not(has_down))
    def _():
        res[2] = jnp.zeros(res.shape[1:], F32)

    def as_int(x):
        return jnp.where(x, 1, 0)

    chips = as_int(has_prev) + as_int(has_next)
    sides = as_int(has_up) + as_int(has_down)
    pl.semaphore_wait(barrier, 1 + 2 * chips + sides * (2 + 2 * chips))

    swap = pltpu.make_async_remote_copy(
        src_ref=slc.at[:, :, :, pl.ds(pl.multiple_of(other * HALF, HALF), HALF)],
        dst_ref=tiles.at[1, pl.ds(2 * c, 2)],
        send_sem=xs,
        recv_sem=xr,
        device_id=device(0, other, 0),
        device_id_type=MESH,
    )
    swap.start()

    def tile_copy(dq, j, core):
        send, recv = (us, ur) if dq < 0 else (vs, vr)
        return pltpu.make_async_remote_copy(
            src_ref=slc.at[j, :, :, pl.ds(core * HALF, HALF)],
            dst_ref=tiles.at[1 - dq, 2 * c + j],
            send_sem=send.at[j, core],
            recv_sem=recv.at[2 * c + j],
            device_id=device(dq, core, 0),
            device_id_type=MESH,
        )

    def send_tiles(dq, j):
        @pl.when(chip_ok(dq))
        def _():
            for core in range(2):
                tile_copy(dq, j, core).start()

    @pl.when(c == 0)
    def _():
        send_tiles(-1, 0)
        send_tiles(-1, 1)
        send_tiles(1, 1)
        send_tiles(1, 0)

    @pl.when(c == 1)
    def _():
        send_tiles(1, 1)
        send_tiles(1, 0)
        send_tiles(-1, 0)
        send_tiles(-1, 1)

    def wait_tile(rel, a):
        recv = ur if rel > 0 else vr

        @pl.when(chip_ok(rel))
        def _():
            pltpu.make_async_copy(tiles.at[1 + rel, a], tiles.at[1 + rel, a], recv.at[a]).wait()

    def reorder(rel, a):
        for part in range(2):
            looks[1 + rel, a, part] = jnp.dot(order, tiles[1 + rel, a, part], preferred_element_type=F32)

    def planes_of(stage):
        return STAGES[stage] + [p for p, _ in BACK[stage]]

    def compute(stage):
        planes = planes_of(stage)
        n = len(planes)

        def lanes(t, carry):
            at = pl.ds(pl.multiple_of(t * CELLS, CELLS), CELLS)
            at2 = pl.ds(pl.multiple_of(t * CELLS + HALF, CELLS), CELLS)

            def total(x):
                return jnp.sum(x.reshape(LOOK_AZ, LOOKS, CELLS), axis=0)

            for i, (kind, u, v) in enumerate(planes):
                ur_, ui_ = looks[1 + u[0], u[1], 0, :, at], looks[1 + u[0], u[1], 1, :, at]
                vr_, vi_ = looks[1 + v[0], v[1], 0, :, at], looks[1 + v[0], v[1], 1, :, at]
                if kind == "pair":
                    x, y = ur_ * vr_ + ui_ * vi_, ui_ * vr_ - ur_ * vi_
                else:
                    x, y = ur_ * ur_ + ui_ * ui_, vr_ * vr_ + vi_ * vi_
                sums[i, :, at] = total(x)
                sums[i, :, at2] = total(y)
            return carry

        lax.fori_loop(0, HALF // CELLS, lanes, 0)
        m = n + n % 2
        if m > n:
            sums[n] = jnp.zeros((LOOKS, WIDTH), F32)
        x = sums[0:m].reshape(m * LOOKS, WIDTH)
        hi = x.astype(BF16)
        lo = (x - hi.astype(F32)).astype(BF16)
        t = table[...]
        out = jnp.dot(hi, t, preferred_element_type=F32) + jnp.dot(lo, t, preferred_element_type=F32)
        out = (out * PLANE_SCALE).reshape(m, LOOKS, CELLS)
        own = len(STAGES[stage])
        res[1, c, STARTS[stage] : STARTS[stage] + own] = out[0:own]
        for i, (_, place) in enumerate(BACK[stage]):
            back[place] = out[own + i]
        if stage == 2:
            for place in BACK_IA:
                back[place] = out[own - 1]
        if stage == 4:
            for place in BACK_IB:
                back[place] = out[own - 1]

    def own_send(stage, target, ds):
        span = pl.ds(STARTS[stage], len(STAGES[stage]))
        k = target if ds != 0 else 2
        return pltpu.make_async_remote_copy(
            src_ref=res.at[1, c, span],
            dst_ref=res.at[1 - ds, c, span],
            send_sem=ps.at[stage, 1 + ds, k],
            recv_sem=pr.at[stage, 1 - ds, c],
            device_id=device(0, other if ds == 0 else target, ds),
            device_id_type=MESH,
        )

    def back_send(m, ds):
        _, core, start, size, place = BACK_SENDS[m]
        return pltpu.make_async_remote_copy(
            src_ref=back.at[pl.ds(start, size)],
            dst_ref=res.at[1 - ds, c, pl.ds(N_OWN + place, size)],
            send_sem=bs.at[m, 1 + ds],
            recv_sem=br.at[m, 1 - ds, c],
            device_id=device(-1, core, ds),
            device_id_type=MESH,
        )

    def all_sends(stage, act):
        for m, spec in enumerate(BACK_SENDS):
            if spec[0] == stage:
                for ds in (0, -1, 1):

                    @when(has_prev, side_ok(ds))
                    def _():
                        act(back_send(m, ds))

        for ds in (-1, 1):

            @when(side_ok(ds))
            def _():
                for target in range(2):
                    act(own_send(stage, target, ds))

        act(own_send(stage, 2, 0))

    own_copy.wait()
    swap.wait_recv()
    for a in range(4):
        reorder(0, a)
    compute(0)
    all_sends(0, lambda copy: copy.start())
    for stage in range(1, 5):
        b, a = stage - 1, 4 - stage
        wait_tile(1, b)
        reorder(1, b)
        wait_tile(-1, a)
        reorder(-1, a)
        compute(stage)
        all_sends(stage, lambda copy: copy.start())

    for stage in range(5):
        span = pl.ds(STARTS[stage], len(STAGES[stage]))
        for ds in (0, -1, 1):
            for h in range(2):
                alive = h != c if ds == 0 else side_ok(ds)

                @pl.when(alive)
                def _():
                    ref = res.at[1 + ds, h, span]
                    pltpu.make_async_copy(ref, ref, pr.at[stage, 1 + ds, h]).wait()

    for m, (_, core, _, size, place) in enumerate(BACK_SENDS):
        for ds in (0, -1, 1):

            @when(has_next, c == core, side_ok(ds))
            def _():
                for h in range(2):
                    ref = res.at[1 + ds, h, pl.ds(N_OWN + place, size)]
                    pltpu.make_async_copy(ref, ref, br.at[m, 1 + ds, h]).wait()

    sub = lax.broadcasted_iota(jnp.int32, (LOOKS, CELLS), 0)
    lane8 = lax.broadcasted_iota(jnp.int32, (LOOKS, CELLS), 1)
    left = lane8 < CELLS // 2

    def rows_box(plane, h):
        before, here, after = res[0, h, plane], res[1, h, plane], res[2, h, plane]
        total = here
        for k in range(1, 4):
            total = total + pltpu.roll(jnp.where(sub >= LOOKS - k, before, here), k, 0)
            total = total + pltpu.roll(jnp.where(sub < k, after, here), LOOKS - k, 0)
        return total

    def low(p0, p1):
        return jnp.where(left, p0, pltpu.roll(p1, CELLS // 2, 1))

    def high(p0, p1):
        return jnp.where(left, pltpu.roll(p0, CELLS // 2, 1), p1)

    def cells_box(x):
        total = x
        for k in range(1, 4):
            total = total + jnp.where(lane8 >= k, pltpu.roll(x, k, 1), 0.0)
            total = total + jnp.where(lane8 < CELLS - k, pltpu.roll(x, CELLS - k, 1), 0.0)
        return total

    for j in range(2):
        a = 2 * c + j
        p = jnp.where(c == 0, 6, 7)
        r0, r1 = rows_box(p, 0), rows_box(p, 1)
        box_ref = cells_box(low(r0, r1) if j == 0 else high(r0, r1))
        for s in range(SLOTS):
            e = second[j, s]
            used = s < count[j]
            off = jnp.clip(e - (4 * q + a), 1, OFFS)
            b = jnp.where(off <= 3 - a, 0, jnp.where(off <= 7 - a, off - (4 - a), off - (8 - a)))
            base = jnp.where(a == 0, 0, jnp.where(a == 1, 3, 5))
            same = base + off - 1
            following = 8 + 4 * b + a + jnp.where(b >= 2, 1, 0)
            far3 = jnp.where(b < 2, b, jnp.where(b == 2, 4, 7))
            far2 = jnp.where(b < 2, 2 + b, 5)
            far = N_OWN + jnp.where(a == 3, far3, jnp.where(a == 2, far2, jnp.where(a == 1, 4 + b, 7)))
            near = off <= 3 - a
            middle = off <= 7 - a
            plane = jnp.where(near, same, jnp.where(middle, following, far))
            e4 = lax.rem(a + off, 4)
            later = e4 >= 2
            sec_near = jnp.where(later, 7, 6)
            sec_mid = jnp.where(later, IB, IA)
            sec_far = N_OWN + jnp.where(later, 8, 6)
            plane_sec = jnp.where(near, sec_near, jnp.where(middle, sec_mid, sec_far))
            odd = lax.rem(a + off, 2) == 1
            p0, p1 = res[1, 0, plane], res[1, 1, plane]
            zero = jnp.zeros((LOOKS, CELLS), F32)
            ifg[j, s, 0] = jnp.where(used, low(p0, p1), zero)
            ifg[j, s, 1] = jnp.where(used, high(p0, p1), zero)
            b0, b1 = rows_box(plane, 0), rows_box(plane, 1)
            s0, s1 = rows_box(plane_sec, 0), rows_box(plane_sec, 1)
            box_r, box_i = cells_box(low(b0, b1)), cells_box(high(b0, b1))
            box_s = cells_box(jnp.where(odd, high(s0, s1), low(s0, s1)))
            value = jnp.sqrt(box_r * box_r + box_i * box_i) / jnp.sqrt(box_ref * box_s)
            coh[j, s] = jnp.where(used, value, zero)

    swap.wait_send()
    for dq in (-1, 1):

        @pl.when(chip_ok(dq))
        def _():
            for j in range(2):
                for core in range(2):
                    tile_copy(dq, j, core).wait_send()

    for stage in range(5):
        all_sends(stage, lambda copy: copy.wait_send())


def shards(slc, pair_second, pair_count):
    dma = pltpu.SemaphoreType.DMA
    hbm = pl.BlockSpec(memory_space=pl.ANY)
    smem = pl.BlockSpec(memory_space=pltpu.SMEM)
    vmem = pl.BlockSpec(memory_space=pltpu.VMEM)
    return pl.pallas_call(
        kernel,
        out_shape=(
            jax.ShapeDtypeStruct((2, SLOTS, 2, LOOKS, CELLS), F32),
            jax.ShapeDtypeStruct((2, SLOTS, LOOKS, CELLS), F32),
        ),
        in_specs=[hbm, smem, smem],
        out_specs=(vmem, vmem),
        scratch_shapes=[
            pltpu.VMEM((3, 4, 2, ROWS, HALF), BF16),
            pltpu.VMEM((3, 4, 2, ROWS, HALF), F32),
            pltpu.VMEM((8, LOOKS, WIDTH), F32),
            pltpu.VMEM((WIDTH, CELLS), BF16),
            pltpu.VMEM((3, 2, N_PLANES, LOOKS, CELLS), F32),
            pltpu.VMEM((N_BACK, LOOKS, CELLS), F32),
            dma,
            dma,
            dma,
            dma((2, 2)),
            dma((4,)),
            dma((2, 2)),
            dma((4,)),
            dma((5, 3, 3)),
            dma((5, 3, 2)),
            dma((5, 3)),
            dma((5, 3, 2)),
        ],
        compiler_params=pltpu.CompilerParams(
            collective_id=0, has_side_effects=True, vmem_limit_bytes=40 * 2**20
        ),
    )(slc, pair_second, pair_count)


def solution(mesh):
    in_specs = (P("date", None, "strip", None), P("date", None), P("date"))
    out_specs = (P("date", None, None, "strip", None), P("date", None, "strip", None))
    return jax.shard_map(shards, mesh=mesh, in_specs=in_specs, out_specs=out_specs, check_vma=False)
```

time: 160 us -> 45.2 us (0.28)
  the two profiles are of different devices: /device:TPU:200 before, /device:TPU:3 now
where the time goes in v1:
time: 45.2 us; the launch traced here: 45.1 us
  Pallas kernels  40.7 us (90%)
  local copies, waits for them, and re-layouts  3.73 us (8%)
  between operations  0.65 us (1%)
    pallas_call x1, Pallas kernels, shards(): pl.pallas_call(kernel, out_shape=(jax.ShapeDtypeStruct((2, SLOTS, 2, LOOK...  40.7 us
    unnamed x8, local copies, waits for them, and re-layouts  3.73 us

profile of v1, /device:TPU:3, one launch (start us, length us, event | category | flops | bytes accessed | tf_op | source)
XLA Modules:
  0.0 45.1 jit_solution(12845228240882036498)
XLA Ops:
  0.6 0.0 copy-start
  0.6 1.1 %copy-done = bf16[2,2,40,2560]{3,2,1,0:T(8,128)(2,1)S(1)} copy-done((bf16[2,2,40,2560]{3,2,1,0:T(8,128)(2,1)S(1)}, bf16[2,2,40,2560]{3,2,1,0:T(8,128)(2,1)}, u32[]{:S(2)}) %copy-start) | copy-done | bytes 819224
  1.8 0.0 copy-start.1
  1.8 0.7 %copy-done.1 = s32[2,6]{1,0:T(2,128)S(1)} copy-done((s32[2,6]{1,0:T(2,128)S(1)}, s32[2,6]{1,0:T(2,128)}, u32[]{:S(2)}) %copy-start.1) | copy-done | bytes 72
  2.5 0.0 copy-start.2
  2.5 0.7 %copy-done.2 = s32[2]{0:T(128)S(1)} copy-done((s32[2]{0:T(128)S(1)}, s32[2]{0:T(128)}, u32[]{:S(2)}) %copy-start.2) | copy-done | bytes 32
  3.1 40.7 %shard_map.50 = (f32[2,6,2,8,128]{4,3,2,1,0:T(8,128)S(1)}, f32[2,6,8,128]{3,2,1,0:T(8,128)S(1)}) custom-call(bf16[2,2,40,2560]{3,2,1,0:T(8,128)(2,1)S(1)} %copy-done, s32[2,6]{1,0:T(2,128)S(1)} %copy-done.1, s32[2]{0:T(128)S(1)} %copy-done.2), custom_call_target="tpu_custom_call" | custom-call | tf_op jit(solution)/shard_map/pallas_call | solution.py:386
  43.8 0.6 %copy.7 = f32[2,6,2,8,128]{4,3,2,1,0:T(8,128)} copy(f32[2,6,2,8,128]{4,3,2,1,0:T(8,128)S(1)} %get-tuple-element.4) | data formatting | bytes 196608
  44.5 0.6 %copy.8 = f32[2,6,8,128]{3,2,1,0:T(8,128)} copy(f32[2,6,8,128]{3,2,1,0:T(8,128)S(1)} %get-tuple-element.5) | data formatting | bytes 98304
Async XLA Ops:
  0.6 1.1 %copy-start = (bf16[2,2,40,2560]{3,2,1,0:T(8,128)(2,1)S(1)}, bf16[2,2,40,2560]{3,2,1,0:T(8,128)(2,1)}, u32[]{:S(2)}) copy-start(bf16[2,2,40,2560]{3,2,1,0:T(8,128)(2,1)} %slc.1) | copy-start | bytes 2457604
  1.8 0.7 %copy-start.1 = (s32[2,6]{1,0:T(2,128)S(1)}, s32[2,6]{1,0:T(2,128)}, u32[]{:S(2)}) copy-start(s32[2,6]{1,0:T(2,128)} %second.1) | copy-start | bytes 148
  2.5 0.7 %copy-start.2 = (s32[2]{0:T(128)S(1)}, s32[2]{0:T(128)}, u32[]{:S(2)}) copy-start(s32[2]{0:T(128)} %count.1) | copy-start | bytes 28

commit v2 on v1

v2 whole, which is shorter than its diff:
```python
import jax
import jax.numpy as jnp
from jax import lax
from jax.experimental import pallas as pl
from jax.experimental.pallas import tpu as pltpu
from jax.sharding import PartitionSpec as P

MESH = pl.DeviceIdType.MESH
F32 = jnp.float32
BF16 = jnp.bfloat16

LOOK_AZ = 5
LOOK_RG = 20
SLOTS = 6
OFFS = 8
CHIPS = 16
STRIPS = 8
ROWS = 40
WIDTH = 2560
HALF = WIDTH // 2
LOOKS = ROWS // LOOK_AZ
CELLS = 128
PLANE_SCALE = 1.0 / (LOOK_AZ * LOOK_RG)


def pair(a, b):
    return ("pair", a, b)


def power(a, b):
    return ("power", a, b)


def onto(b, *middle):
    return [pair((0, 0), (1, b)), pair((0, 1), (1, b)), *middle, pair((0, 2), (1, b)), pair((0, 3), (1, b))]


NEXT = [(0, 2), (2, 0), (1, 3), (3, 1)]
PREV = [(1, 3), (3, 1), (0, 2), (2, 0)]
SAME = [(0, 1), (0, 2), (0, 3), (1, 2), (1, 3)]
STAGES = [
    [pair((0, a), (0, b)) for a, b in SAME] + [power((0, 0), (0, 2)), power((0, 1), (0, 3)), pair((0, 2), (0, 3))],
    onto(NEXT[0]),
    onto(NEXT[1], power((1, 0), (1, 2))),
    onto(NEXT[2]),
    onto(NEXT[3], power((1, 1), (1, 3))),
]
STARTS = [0, 8, 12, 17, 21]
NEEDS = [[(0, 7), (5, 3)], [(0, 2), (2, 2)], [(0, 3), (2, 3)], [(0, 2), (2, 2)], [(0, 3), (2, 3)]]
N_OWN = 26
BACK = [
    [],
    [(((1, 0), 0), ((3, 2), 2))],
    [(((3, 0), 4), ((3, 0), 3)), (((3, 2), 5), ((1, 0), 0))],
    [(((0, 0), 1), ((3, 3), 4)), (((1, 1), 2), ((2, 0), 5)), (((3, 1), 6), ((2, 2), 6))],
    [(((2, 0), 10), ((3, 1), 12)), (((2, 2), 11), ((2, 1), 13)), (((2, 1), 12), ((1, 1), 9)), (((3, 3), 13), ((0, 0), 10))],
]
BACK_POWER = {2: [(3, 7), (1, 7)], 4: [(8, 9), (8, 11)]}
N_BACK = 14
BACK_SENDS = [
    (3, 0, 0, 0, 4),
    (3, 0, 1, 4, 4),
    (3, 1, 0, 0, 2),
    (3, 1, 1, 2, 6),
    (4, 0, 0, 8, 1),
    (4, 0, 1, 9, 5),
    (4, 1, 0, 8, 3),
    (4, 1, 1, 11, 3),
]
FAR = [{}, {}]
for stage_ in BACK:
    for both_ in stage_:
        for core_ in range(2):
            FAR[core_][both_[core_][0]] = both_[core_][1]
N_PLANES = N_OWN + N_BACK


def when(*conditions):
    conditions = [x for x in conditions if x is not None]
    if not conditions:
        return lambda f: f()
    total = conditions[0]
    for x in conditions[1:]:
        total = jnp.logical_and(total, x)
    return pl.when(total)


def planes_kernel(
    slc, second_in, count_in, ifg, coh, res, edge, tiles, looks, sums, table, back, rim, back_rim, second, count,
    lsem, sem2, xs, xr, us, ur, vs, vr, fs, ps, pr, hs, hr, bs, br,
):
    date = lax.axis_index("date")
    strip = lax.axis_index("strip")
    q = date // 2
    c = date % 2
    other = 1 - c
    has_prev, has_next = q > 0, q < CHIPS - 1
    has_up, has_down = strip > 0, strip < STRIPS - 1

    def device(dq, core, ds):
        return ((q + dq) * 2 + core, strip + ds)

    def side_ok(ds):
        return {0: None, -1: has_up, 1: has_down}[ds]

    def chip_ok(dq):
        return {0: None, -1: has_prev, 1: has_next}[dq]

    def by_core(x):
        if isinstance(x, tuple):
            return jnp.where(c == 0, x[0], x[1])
        return x

    own_copy = pltpu.make_async_copy(
        slc.at[:, :, :, pl.ds(pl.multiple_of(c * HALF, HALF), HALF)], tiles.at[1, pl.ds(2 * c, 2)], lsem
    )
    own_copy.start()
    second_copy = pltpu.make_async_copy(second_in, second, sem2.at[0])
    count_copy = pltpu.make_async_copy(count_in, count, sem2.at[1])
    second_copy.start()
    count_copy.start()

    barrier = pltpu.get_barrier_semaphore()
    for dq in (-1, 1):

        @when(chip_ok(dq))
        def _():
            for core in range(2):
                pl.semaphore_signal(barrier, inc=1, device_id=device(dq, core, 0), device_id_type=MESH)

    pl.semaphore_signal(barrier, inc=1, device_id=device(0, other, 0), device_id_type=MESH)
    for ds in (-1, 1):

        @when(side_ok(ds))
        def _():
            pl.semaphore_signal(barrier, inc=1, device_id=device(0, c, ds), device_id_type=MESH)

    last, mid = CHIPS - 1, CHIPS // 2

    def hello(chip, cores):
        for core in cores:
            pl.semaphore_signal(barrier, inc=1, device_id=(chip * 2 + core, strip), device_id_type=MESH)

    pl.when(q == 0)(lambda: hello(mid, (0, 1)))
    pl.when(q == mid - 1)(lambda: hello(0, (c,)))
    pl.when(q == last)(lambda: hello(mid - 1, (0, 1)))
    pl.when(q == mid)(lambda: hello(last, (c,)))

    def as_int(x):
        return jnp.where(x, 1, 0)

    relays = jnp.logical_or(q == 0, q == last)
    relayed = jnp.logical_or(q == mid - 1, q == mid)
    greeted = 1 + 2 * (as_int(has_prev) + as_int(has_next)) + as_int(has_up) + as_int(has_down)
    pl.semaphore_wait(barrier, greeted + as_int(relays) + 2 * as_int(relayed))

    swap = pltpu.make_async_remote_copy(
        src_ref=slc.at[:, :, :, pl.ds(pl.multiple_of(other * HALF, HALF), HALF)],
        dst_ref=tiles.at[1, pl.ds(2 * c, 2)],
        send_sem=xs,
        recv_sem=xr,
        device_id=device(0, other, 0),
        device_id_type=MESH,
    )

    def tile_copy(dq, j, core, relay):
        send, recv = (us, ur) if dq < 0 else (vs, vr)
        chip = q + dq
        if relay:
            chip = 0 if dq < 0 else last
        if relay:
            recv = vr if dq < 0 else ur
        return pltpu.make_async_remote_copy(
            src_ref=slc.at[j, :, :, pl.ds(core * HALF, HALF)],
            dst_ref=tiles.at[1 + dq if relay else 1 - dq, 2 * c + j],
            send_sem=send.at[j, core],
            recv_sem=recv.at[2 * c + j],
            device_id=(chip * 2 + core, strip),
            device_id_type=MESH,
        )

    def forward_copy(a, side, recv, chip, step):
        return pltpu.make_async_remote_copy(
            src_ref=tiles.at[2 - side, a],
            dst_ref=tiles.at[side, a],
            send_sem=fs.at[step],
            recv_sem=recv.at[a],
            device_id=(chip * 2 + c, strip),
            device_id_type=MESH,
        )

    def pass_on(step):
        def one(a, side, came, recv, chip):
            pltpu.make_async_copy(tiles.at[2 - side, a], tiles.at[2 - side, a], came.at[a]).wait()
            forward_copy(a, side, recv, chip, step).start()

        pl.when(q == 0)(lambda: one(by_core(NEXT[2 + step]), 2, vr, ur, mid - 1))
        pl.when(q == last)(lambda: one(by_core(PREV[2 + step]), 0, ur, vr, mid))

    def passed_on(step):
        pl.when(q == 0)(lambda: forward_copy(by_core(NEXT[2 + step]), 2, ur, mid - 1, step).wait_send())
        pl.when(q == last)(lambda: forward_copy(by_core(PREV[2 + step]), 0, vr, mid, step).wait_send())

    def tile_sends(act):
        for here in range(2):

            @pl.when(c == here)
            def _():
                for n in range(4):
                    for dq in (-1, 1):
                        j = n // 2 if dq < 0 else 1 - n // 2
                        core = (here + n) % 2

                        far = q == (mid if dq < 0 else mid - 1)
                        if n < 2:
                            when(chip_ok(dq))(lambda: act(tile_copy(dq, j, core, False)))
                        else:
                            when(chip_ok(dq), jnp.logical_not(far))(lambda: act(tile_copy(dq, j, core, False)))
                            when(far)(lambda: act(tile_copy(dq, j, core, True)))

    def start(copy):
        copy.start()

    def wait_send(copy):
        copy.wait_send()

    swap.start()
    tile_sends(start)

    first = lax.broadcasted_iota(jnp.int32, (CELLS, CELLS), 1) * LOOK_RG
    lane = lax.broadcasted_iota(jnp.int32, (CELLS, CELLS), 0)

    def fill(i, carry):
        delta = lane + i * CELLS - first
        inside = jnp.logical_and(delta >= 0, delta < LOOK_RG)
        table[pl.ds(pl.multiple_of(i * CELLS, CELLS), CELLS), :] = jnp.where(inside, 1.0, 0.0).astype(BF16)
        return carry

    lax.fori_loop(0, WIDTH // CELLS, fill, 0)
    row = lax.broadcasted_iota(jnp.int32, (ROWS, ROWS), 0)
    col = lax.broadcasted_iota(jnp.int32, (ROWS, ROWS), 1)
    order = jnp.where(col == LOOK_AZ * (row % LOOKS) + row // LOOKS, 1.0, 0.0).astype(BF16)
    sub = lax.broadcasted_iota(jnp.int32, (LOOKS, CELLS), 0)
    lane8 = lax.broadcasted_iota(jnp.int32, (LOOKS, CELLS), 1)
    left = lane8 < CELLS // 2

    @pl.when(jnp.logical_not(has_up))
    def _():
        edge[0] = jnp.zeros(edge.shape[1:], F32)

    @pl.when(jnp.logical_not(has_down))
    def _():
        edge[1] = jnp.zeros(edge.shape[1:], F32)

    def wait_tile(rel, a):
        recv = ur if rel > 0 else vr

        @when(chip_ok(rel))
        def _():
            pltpu.make_async_copy(tiles.at[1 + rel, a], tiles.at[1 + rel, a], recv.at[a]).wait()

    def reorder(rel, a):
        @when(chip_ok(rel))
        def _():
            for part in range(2):
                looks[1 + rel, a, part] = jnp.dot(order, tiles[1 + rel, a, part], preferred_element_type=F32)

    def rims(x):
        d = jnp.where(sub < 3, pltpu.roll(x, 3, 0), 0.0)
        d = d + pltpu.roll(d, LOOKS - 1, 0) + pltpu.roll(d, LOOKS - 2, 0)
        u = jnp.where(jnp.logical_and(sub >= 1, sub < 4), pltpu.roll(x, 1, 0), 0.0)
        u = u + pltpu.roll(u, 1, 0) + pltpu.roll(u, 2, 0)
        return d[0:4], u[0:4]

    def compute(stage):
        planes = list(STAGES[stage])
        for (pair0, _), (pair1, _) in BACK[stage]:
            planes.append(pair((-1, (pair0[0], pair1[0])), (1, (pair0[1], pair1[1]))))
        planes = [(kind, (u[0], by_core(u[1])), (v[0], by_core(v[1]))) for kind, u, v in planes]
        n = len(planes)

        def lanes(t, carry):
            at = pl.ds(pl.multiple_of(t * CELLS, CELLS), CELLS)
            at2 = pl.ds(pl.multiple_of(t * CELLS + HALF, CELLS), CELLS)

            def total(x):
                return jnp.sum(x.reshape(LOOK_AZ, LOOKS, CELLS), axis=0)

            for i, (kind, u, v) in enumerate(planes):
                u_r, u_i = looks[1 + u[0], u[1], 0, :, at], looks[1 + u[0], u[1], 1, :, at]
                v_r, v_i = looks[1 + v[0], v[1], 0, :, at], looks[1 + v[0], v[1], 1, :, at]
                if kind == "pair":
                    x, y = u_r * v_r + u_i * v_i, u_i * v_r - u_r * v_i
                else:
                    x, y = u_r * u_r + u_i * u_i, v_r * v_r + v_i * v_i
                sums[i, :, at] = total(x)
                sums[i, :, at2] = total(y)
            return carry

        lax.fori_loop(0, HALF // CELLS, lanes, 0)
        m = n + n % 2
        if m > n:
            sums[n] = jnp.zeros((LOOKS, WIDTH), F32)
        x = sums[0:m].reshape(m * LOOKS, WIDTH)
        hi = x.astype(BF16)
        lo = (x - hi.astype(F32)).astype(BF16)
        t = table[...]
        out = jnp.dot(hi, t, preferred_element_type=F32) + jnp.dot(lo, t, preferred_element_type=F32)
        out = (out * PLANE_SCALE).reshape(m, LOOKS, CELLS)
        own = len(STAGES[stage])
        for i in range(own):
            res[c, STARTS[stage] + i] = out[i]
            rim[0, STARTS[stage] + i], rim[1, STARTS[stage] + i] = rims(out[i])
        places = [(own + i, (p0, p1)) for i, ((_, p0), (_, p1)) in enumerate(BACK[stage])]
        if stage in BACK_POWER:
            places += [(2, (p0, p1)) for p0, p1 in zip(*BACK_POWER[stage], strict=True)]
        for i, place in places:
            place = by_core(place)
            back[place] = out[i]
            back_rim[0, place], back_rim[1, place] = rims(out[i])

    def span_of(stage, core):
        if stage == 0:
            return pl.ds(0, 8)
        return pl.ds(STARTS[stage] + 2 * core, NEEDS[stage][0][1])

    def core_send(stage):
        return pltpu.make_async_remote_copy(
            src_ref=res.at[c, span_of(stage, other)],
            dst_ref=res.at[c, span_of(stage, other)],
            send_sem=ps.at[stage],
            recv_sem=pr.at[stage],
            device_id=device(0, other, 0),
            device_id_type=MESH,
        )

    def rim_send(stage, core, ds):
        first_, size = NEEDS[stage][core]
        side = (1 - ds) // 2
        span = pl.ds(STARTS[stage] + first_, size)
        return pltpu.make_async_remote_copy(
            src_ref=rim.at[side, span],
            dst_ref=edge.at[side, c, span],
            send_sem=hs.at[stage, core, side],
            recv_sem=hr.at[stage, c, side],
            device_id=device(0, core, ds),
            device_id_type=MESH,
        )

    def back_send(m, ds):
        _, _, core, first_, size = BACK_SENDS[m]
        span, there = pl.ds(first_, size), pl.ds(N_OWN + first_, size)
        if ds == 0:
            src, dst = back.at[span], res.at[c, there]
        else:
            side = (1 - ds) // 2
            src, dst = back_rim.at[side, span], edge.at[side, c, there]
        return pltpu.make_async_remote_copy(
            src_ref=src,
            dst_ref=dst,
            send_sem=bs.at[m, 1 + ds],
            recv_sem=br.at[m, 1 + ds],
            device_id=device(-1, core, ds),
            device_id_type=MESH,
        )

    def all_sends(stage, act):
        for here in range(2):
            specs = [m for m, spec in enumerate(BACK_SENDS) if spec[0] == stage and spec[1] == here]
            if specs:

                @when(c == here, has_prev)
                def _():
                    for ds in (-1, 1, 0):

                        @when(side_ok(ds))
                        def _():
                            for m in specs:
                                act(back_send(m, ds))

        for ds in (-1, 1):

            @when(side_ok(ds))
            def _():
                for core in range(2):
                    act(rim_send(stage, core, ds))

        act(core_send(stage))

    def own_arrivals(stage):
        ref = res.at[other, span_of(stage, c)]
        pltpu.make_async_copy(ref, ref, pr.at[stage]).wait()
        for ds in (-1, 1):
            side = (1 - ds) // 2
            for core in range(2):
                first_, size = NEEDS[stage][core]

                @when(side_ok(-ds), c == core)
                def _():
                    for h in range(2):
                        ref = edge.at[side, h, pl.ds(STARTS[stage] + first_, size)]
                        pltpu.make_async_copy(ref, ref, hr.at[stage, h, side]).wait()

    def back_arrivals(stage):
        for core in range(2):
            for ds in (0, -1, 1):

                @when(has_next, c == core, side_ok(-ds))
                def _():
                    for m, (after, h, to, first_, size) in enumerate(BACK_SENDS):
                        if after == stage and to == core:
                            span = pl.ds(N_OWN + first_, size)
                            ref = res.at[h, span] if ds == 0 else edge.at[(1 - ds) // 2, h, span]
                            pltpu.make_async_copy(ref, ref, br.at[m, 1 + ds]).wait()

    own_copy.wait()
    second_copy.wait()
    count_copy.wait()
    swap.wait_recv()
    for a in range(4):
        reorder(0, a)
    compute(0)
    all_sends(0, start)
    swap.wait_send()
    for stage in range(1, 5):
        b, a = by_core(NEXT[stage - 1]), by_core(PREV[stage - 1])
        wait_tile(1, b)
        reorder(1, b)
        wait_tile(-1, a)
        reorder(-1, a)
        compute(stage)
        all_sends(stage, start)
        if stage <= 2:
            pass_on(stage - 1)
        all_sends(stage - 1, wait_send)
        own_arrivals(stage - 1)
    tile_sends(wait_send)
    for step in range(2):
        passed_on(step)
    back_arrivals(3)
    own_arrivals(4)
    back_arrivals(4)

    def low(p0, p1):
        return jnp.where(left, p0, pltpu.roll(p1, CELLS // 2, 1))

    def high(p0, p1):
        return jnp.where(left, pltpu.roll(p0, CELLS // 2, 1), p1)

    def rows_box(h, plane):
        x = res[h, plane]
        total = x + jnp.concatenate([edge[0, h, plane], edge[1, h, plane]], axis=0)
        for k in range(1, 4):
            total = total + jnp.where(sub >= k, pltpu.roll(x, k, 0), 0.0)
            total = total + jnp.where(sub < LOOKS - k, pltpu.roll(x, LOOKS - k, 0), 0.0)
        return total

    def cells_box(x):
        total = x
        for k in range(1, 4):
            total = total + jnp.where(lane8 >= k, pltpu.roll(x, k, 1), 0.0)
            total = total + jnp.where(lane8 < CELLS - k, pltpu.roll(x, CELLS - k, 1), 0.0)
        return total

    def table_of(a, b, entries):
        value = 0
        for (ea, eb), place in entries.items():
            value = jnp.where(jnp.logical_and(a == ea, b == eb), place, value)
        return value

    zero = jnp.zeros((LOOKS, CELLS), F32)
    for j in range(2):
        a = 2 * c + j
        p = 5 + j
        r0, r1 = rows_box(0, p), rows_box(1, p)
        box_ref = cells_box(jnp.where(c == 0, low(r0, r1), high(r0, r1)))
        for s in range(SLOTS):
            used = s < count[j]
            off = jnp.clip(second[j, s] - (4 * q + a), 1, OFFS)
            near, middle = off <= 3 - a, off <= 7 - a
            e = lax.rem(a + off, 4)
            same = off - 1 + jnp.where(a == 0, 0, jnp.where(a == 1, 3, 7))
            planes, secs = [], []
            for h in range(2):
                here = e if h == 0 else jnp.where(e >= 2, e - 2, e + 2)
                step = jnp.where(here == 1, 2, jnp.where(here == 2, 1, here))
                up = jnp.where(jnp.logical_and(lax.rem(step, 2) == 1, a >= 2), 1, 0)
                following = 8 + 4 * step + jnp.where(step >= 2, 1, 0) + a + up
                far = N_OWN + table_of(a, e, FAR[h])
                planes.append(jnp.where(near, same, jnp.where(middle, following, far)))
                power2 = BACK_POWER[2][h]
                power4 = BACK_POWER[4][h]
                far_even = N_OWN + jnp.where(c == 0, power2[0], power2[1])
                far_odd = N_OWN + jnp.where(c == 0, power4[0], power4[1])
                sec_even = jnp.where(near, 5, jnp.where(middle, 14, far_even))
                sec_odd = jnp.where(near, 6, jnp.where(middle, 23, far_odd))
                secs.append(jnp.where(lax.rem(e, 2) == 1, sec_odd, sec_even))
            p0, p1 = res[0, planes[0]], res[1, planes[1]]
            ifg[j, s, 0] = jnp.where(used, low(p0, p1), zero)
            ifg[j, s, 1] = jnp.where(used, high(p0, p1), zero)
            b0, b1 = rows_box(0, planes[0]), rows_box(1, planes[1])
            s0, s1 = rows_box(0, secs[0]), rows_box(1, secs[1])
            box_r, box_i = cells_box(low(b0, b1)), cells_box(high(b0, b1))
            box_s = cells_box(jnp.where(e >= 2, high(s0, s1), low(s0, s1)))
            value = jnp.sqrt(box_r * box_r + box_i * box_i) / jnp.sqrt(box_ref * box_s)
            coh[j, s] = jnp.where(used, value, zero)

    all_sends(4, wait_send)


def store_kernel(ifg, coh, ifg_out, coh_out, sems):
    copies = [
        pltpu.make_async_copy(ifg, ifg_out, sems.at[0]),
        pltpu.make_async_copy(coh, coh_out, sems.at[1]),
    ]
    for copy in copies:
        copy.start()
    for copy in copies:
        copy.wait()


def shards(slc, pair_second, pair_count):
    dma = pltpu.SemaphoreType.DMA
    hbm = pl.BlockSpec(memory_space=pltpu.HBM)
    vmem = pl.BlockSpec(memory_space=pltpu.VMEM)
    ifg_shape = (2, SLOTS, 2, LOOKS, CELLS)
    coh_shape = (2, SLOTS, LOOKS, CELLS)
    operands = [pltpu.with_memory_space_constraint(x, pltpu.HBM) for x in (slc, pair_second, pair_count)]
    ifg, coh = pl.pallas_call(
        planes_kernel,
        out_shape=(pltpu.VMEM(ifg_shape, F32), pltpu.VMEM(coh_shape, F32)),
        in_specs=[hbm, hbm, hbm],
        out_specs=(vmem, vmem),
        scratch_shapes=[
            pltpu.VMEM((2, N_PLANES, LOOKS, CELLS), F32),
            pltpu.VMEM((2, 2, N_PLANES, 4, CELLS), F32),
            pltpu.VMEM((3, 4, 2, ROWS, HALF), BF16),
            pltpu.VMEM((3, 4, 2, ROWS, HALF), F32),
            pltpu.VMEM((10, LOOKS, WIDTH), F32),
            pltpu.VMEM((WIDTH, CELLS), BF16),
            pltpu.VMEM((N_BACK, LOOKS, CELLS), F32),
            pltpu.VMEM((2, N_OWN, 4, CELLS), F32),
            pltpu.VMEM((2, N_BACK, 4, CELLS), F32),
            pltpu.SMEM((2, SLOTS), jnp.int32),
            pltpu.SMEM((2,), jnp.int32),
            dma,
            dma((2,)),
            dma,
            dma,
            dma((2, 2)),
            dma((4,)),
            dma((2, 2)),
            dma((4,)),
            dma((2,)),
            dma((5,)),
            dma((5,)),
            dma((5, 2, 2)),
            dma((5, 2, 2)),
            dma((8, 3)),
            dma((8, 3)),
        ],
        compiler_params=pltpu.CompilerParams(
            collective_id=0, has_side_effects=True, vmem_limit_bytes=40 * 2**20
        ),
    )(*operands)
    return pl.pallas_call(
        store_kernel,
        out_shape=(jax.ShapeDtypeStruct(ifg_shape, F32), jax.ShapeDtypeStruct(coh_shape, F32)),
        in_specs=[vmem, vmem],
        out_specs=(pl.BlockSpec(memory_space=pl.ANY), pl.BlockSpec(memory_space=pl.ANY)),
        scratch_shapes=[dma((2,))],
        compiler_params=pltpu.CompilerParams(vmem_limit_bytes=16 * 2**20),
    )(ifg, coh)


def solution(mesh):
    in_specs = (P("date", None, "strip", None), P("date", None), P("date"))
    out_specs = (P("date", None, None, "strip", None), P("date", None, "strip", None))
    return jax.shard_map(shards, mesh=mesh, in_specs=in_specs, out_specs=out_specs, check_vma=False)
```

time: 45.2 us -> 37 us (0.82)
  the two profiles are of different devices: /device:TPU:3 before, /device:TPU:25 now
where the time goes in v2:
time: 37 us; the launch traced here: 36.9 us
  Pallas kernels  36.3 us (98%)
  between operations  0.64 us (2%)
    pallas_call x1, Pallas kernels, shards(): pl.pallas_call(planes_kernel, out_shape=(pltpu.VMEM(ifg_shape, F32), pltp...  35.6 us

profile of v2, /device:TPU:25, one launch (start us, length us, event | category | flops | bytes accessed | tf_op | source)
XLA Modules:
  0.0 36.9 jit_solution(14257502598187240152)
XLA Ops:
  0.6 35.6 %shard_map.50 = (f32[2,6,2,8,128]{4,3,2,1,0:T(8,128)S(1)}, f32[2,6,8,128]{3,2,1,0:T(8,128)S(1)}) custom-call(bf16[2,2,40,2560]{3,2,1,0:T(8,128)(2,1)} %slc.1, s32[2,6]{1,0:T(2,128)} %second_in.1, s32[2]{0:T(128)} %count_in.1), custom_call_target="tpu_custom_call" | custom-call | tf_op jit(solution)/shard_map/pallas_call | solution.py:529
  36.2 0.7 %shard_map.51 = (f32[2,6,2,8,128]{4,3,2,1,0:T(8,128)}, f32[2,6,8,128]{3,2,1,0:T(8,128)}) custom-call(f32[2,6,2,8,128]{4,3,2,1,0:T(8,128)S(1)} %get-tuple-element.4.ifg, f32[2,6,8,128]{3,2,1,0:T(8,128)S(1)} %get-tuple-element.5.coh), custom_call_target="tpu_custom_call" | custom-call | tf_op jit(solution)/shard_map/pallas_call | solution.py:566

commit v3 on v2

--- a/solution.py
+++ b/solution.py
@@ -48,6 +48,7 @@
 STARTS = [0, 8, 12, 17, 21]
 NEEDS = [[(0, 7), (5, 3)], [(0, 2), (2, 2)], [(0, 3), (2, 3)], [(0, 2), (2, 2)], [(0, 3), (2, 3)]]
 N_OWN = 26
+IA, IB = 14, 23
 BACK = [
     [],
     [(((1, 0), 0), ((3, 2), 2))],
@@ -75,6 +76,36 @@
 N_PLANES = N_OWN + N_BACK
 
 
+def arrival(b, core):
+    return 1 + [x[core] for x in NEXT].index(b)
+
+
+def finals(core, when_):
+    found = []
+    for j in range(2):
+        a = 2 * core + j
+        for off in range(1, OFFS + 1):
+            chip, e = divmod(a + off, 4)
+            odd, half = e % 2, e // 2
+            if chip == 0:
+                step, place = 0, [(SAME + [None, None, (2, 3)]).index((a, e))] * 2
+                sec = [6 if odd else 5] * 2
+            elif chip == 1:
+                step, place = 2 if odd else 1, []
+                for h in range(2):
+                    t = arrival(e, h)
+                    place.append(STARTS[t] + a + (1 if t % 2 == 0 and a >= 2 else 0))
+                sec = [IB if odd else IA] * 2
+            else:
+                place = [N_OWN + FAR[h][(a, e)] for h in range(2)]
+                late = any(spec[0] == 4 and spec[1] == h and spec[3] <= FAR[h][(a, e)] < spec[3] + spec[4] for spec in BACK_SENDS for h in range(2))
+                step = 4 if late or odd else 3
+                sec = [N_OWN + BACK_POWER[4 if odd else 2][h][core] for h in range(2)]
+            if step == when_:
+                found.append((j, off, place, sec, half))
+    return found
+
+
 def when(*conditions):
     conditions = [x for x in conditions if x is not None]
     if not conditions:
@@ -86,8 +117,8 @@
 
 
 def planes_kernel(
-    slc, second_in, count_in, ifg, coh, res, edge, tiles, looks, sums, table, back, rim, back_rim, second, count,
-    lsem, sem2, xs, xr, us, ur, vs, vr, fs, ps, pr, hs, hr, bs, br,
+    slc, second_in, count_in, ifg, coh, res, edge, tiles, looks, sums, table, back, rim, back_rim, second, count, every_ifg, every_coh, box_ref,
+    lsem, sem2, xs, xr, us, ur, vs, vr, us2, ur2, vs2, vr2, fs, ps, pr, hs, hr, bs, br,
 ):
     date = lax.axis_index("date")
     strip = lax.axis_index("strip")
@@ -163,43 +194,64 @@
         device_id_type=MESH,
     )
 
-    def tile_copy(dq, j, core, relay):
-        send, recv = (us, ur) if dq < 0 else (vs, vr)
+    def tile_copy(dq, j, core, relay, part):
+        send, recv = (us.at[j, core], ur) if dq < 0 else (vs.at[j, core], vr)
+        if part == 1:
+            send = us2 if dq < 0 else vs2
         chip = q + dq
         if relay:
             chip = 0 if dq < 0 else last
         if relay:
             recv = vr if dq < 0 else ur
+        if part == 1:
+            recv = {0: ur2, 1: vr2}[0 if recv is ur else 1]
+        start_, width = (0, HALF) if part is None else (part * HALF // 2, HALF // 2)
         return pltpu.make_async_remote_copy(
-            src_ref=slc.at[j, :, :, pl.ds(core * HALF, HALF)],
-            dst_ref=tiles.at[1 + dq if relay else 1 - dq, 2 * c + j],
-            send_sem=send.at[j, core],
+            src_ref=slc.at[j, :, :, pl.ds(core * HALF + start_, width)],
+            dst_ref=tiles.at[1 + dq if relay else 1 - dq, 2 * c + j, :, :, pl.ds(start_, width)],
+            send_sem=send,
             recv_sem=recv.at[2 * c + j],
             device_id=(chip * 2 + core, strip),
             device_id_type=MESH,
         )
 
-    def forward_copy(a, side, recv, chip, step):
-        return pltpu.make_async_remote_copy(
-            src_ref=tiles.at[2 - side, a],
-            dst_ref=tiles.at[side, a],
-            send_sem=fs.at[step],
+    PARTS = [(0, None), (1, 0), (1, 1)]
+
+    def part_of(ref, part):
+        if part is None:
+            return ref
+        return ref.at[:, :, pl.ds(part * HALF // 2, HALF // 2)]
+
+    def forward_copy(n, at_first):
+        step, part = PARTS[n]
+        a = by_core((NEXT if at_first else PREV)[2 + step])
+        side = 2 if at_first else 0
+        came, recv = (vr, ur) if at_first else (ur, vr)
+        if part == 1:
+            came, recv = (vr2, ur2) if at_first else (ur2, vr2)
+        here = part_of(tiles.at[2 - side, a], part)
+        copy = pltpu.make_async_remote_copy(
+            src_ref=here,
+            dst_ref=part_of(tiles.at[side, a], part),
+            send_sem=fs.at[n],
             recv_sem=recv.at[a],
-            device_id=(chip * 2 + c, strip),
+            device_id=((mid - 1 if at_first else mid) * 2 + c, strip),
             device_id_type=MESH,
         )
-
-    def pass_on(step):
-        def one(a, side, came, recv, chip):
-            pltpu.make_async_copy(tiles.at[2 - side, a], tiles.at[2 - side, a], came.at[a]).wait()
-            forward_copy(a, side, recv, chip, step).start()
-
-        pl.when(q == 0)(lambda: one(by_core(NEXT[2 + step]), 2, vr, ur, mid - 1))
-        pl.when(q == last)(lambda: one(by_core(PREV[2 + step]), 0, ur, vr, mid))
-
-    def passed_on(step):
-        pl.when(q == 0)(lambda: forward_copy(by_core(NEXT[2 + step]), 2, ur, mid - 1, step).wait_send())
-        pl.when(q == last)(lambda: forward_copy(by_core(PREV[2 + step]), 0, vr, mid, step).wait_send())
+        return here, came.at[a], copy
+
+    def pass_on(n):
+        def one(at_first):
+            here, came, copy = forward_copy(n, at_first)
+            pltpu.make_async_copy(here, here, came).wait()
+            copy.start()
+
+        pl.when(q == 0)(lambda: one(True))
+        pl.when(q == last)(lambda: one(False))
+
+    def passed_on(n):
+        pl.when(q == 0)(lambda: forward_copy(n, True)[2].wait_send())
+        pl.when(q == last)(lambda: forward_copy(n, False)[2].wait_send())
 
     def tile_sends(act):
         for here in range(2):
@@ -212,11 +264,16 @@
                         core = (here + n) % 2
 
                         far = q == (mid if dq < 0 else mid - 1)
+
+                        def send_parts(relay):
+                            for part in (0, 1) if n == 3 else (None,):
+                                act(tile_copy(dq, j, core, relay, part))
+
                         if n < 2:
-                            when(chip_ok(dq))(lambda: act(tile_copy(dq, j, core, False)))
+                            when(chip_ok(dq))(lambda: send_parts(False))
                         else:
-                            when(chip_ok(dq), jnp.logical_not(far))(lambda: act(tile_copy(dq, j, core, False)))
-                            when(far)(lambda: act(tile_copy(dq, j, core, True)))
+                            when(chip_ok(dq), jnp.logical_not(far))(lambda: send_parts(False))
+                            when(far)(lambda: send_parts(True))
 
     def start(copy):
         copy.start()
@@ -252,18 +309,18 @@
     def _():
         edge[1] = jnp.zeros(edge.shape[1:], F32)
 
-    def wait_tile(rel, a):
-        recv = ur if rel > 0 else vr
-
+    def get_tile(rel, a, part):
         @when(chip_ok(rel))
         def _():
-            pltpu.make_async_copy(tiles.at[1 + rel, a], tiles.at[1 + rel, a], recv.at[a]).wait()
-
-    def reorder(rel, a):
-        @when(chip_ok(rel))
-        def _():
-            for part in range(2):
-                looks[1 + rel, a, part] = jnp.dot(order, tiles[1 + rel, a, part], preferred_element_type=F32)
+            whole, second_half = (ur, ur2) if rel > 0 else (vr, vr2)
+            ref = part_of(tiles.at[1 + rel, a], part)
+            pltpu.make_async_copy(ref, ref, (second_half if part == 1 else whole).at[a]).wait()
+            reorder(rel, a, part)
+
+    def reorder(rel, a, part):
+        at = slice(None) if part is None else pl.ds(part * HALF // 2, HALF // 2)
+        for i in range(2):
+            looks[1 + rel, a, i, :, at] = jnp.dot(order, tiles[1 + rel, a, i, :, at], preferred_element_type=F32)
 
     def rims(x):
         d = jnp.where(sub < 3, pltpu.roll(x, 3, 0), 0.0)
@@ -272,12 +329,16 @@
         u = u + pltpu.roll(u, 1, 0) + pltpu.roll(u, 2, 0)
         return d[0:4], u[0:4]
 
-    def compute(stage):
-        planes = list(STAGES[stage])
-        for (pair0, _), (pair1, _) in BACK[stage]:
-            planes.append(pair((-1, (pair0[0], pair1[0])), (1, (pair0[1], pair1[1]))))
-        planes = [(kind, (u[0], by_core(u[1])), (v[0], by_core(v[1]))) for kind, u, v in planes]
+    def planes_of(stage, own, far):
+        planes = list(STAGES[stage]) if own else []
+        if far:
+            for (pair0, _), (pair1, _) in BACK[stage]:
+                planes.append(pair((-1, (pair0[0], pair1[0])), (1, (pair0[1], pair1[1]))))
+        return [(kind, (u[0], by_core(u[1])), (v[0], by_core(v[1]))) for kind, u, v in planes]
+
+    def looked(planes, at0, part):
         n = len(planes)
+        m = n + n % 2
 
         def lanes(t, carry):
             at = pl.ds(pl.multiple_of(t * CELLS, CELLS), CELLS)
@@ -293,31 +354,52 @@
                     x, y = u_r * v_r + u_i * v_i, u_i * v_r - u_r * v_i
                 else:
                     x, y = u_r * u_r + u_i * u_i, v_r * v_r + v_i * v_i
-                sums[i, :, at] = total(x)
-                sums[i, :, at2] = total(y)
+                sums[at0 + i, :, at] = total(x)
+                sums[at0 + i, :, at2] = total(y)
             return carry
 
-        lax.fori_loop(0, HALF // CELLS, lanes, 0)
-        m = n + n % 2
+        steps = HALF // CELLS
+        spans = [(0, WIDTH)]
+        first_, end = 0, steps
+        if part is not None:
+            spans = [(part * HALF // 2, HALF // 2), (HALF + part * HALF // 2, HALF // 2)]
+            first_, end = part * steps // 2, (part + 1) * steps // 2
+        lax.fori_loop(first_, end, lanes, 0)
         if m > n:
-            sums[n] = jnp.zeros((LOOKS, WIDTH), F32)
-        x = sums[0:m].reshape(m * LOOKS, WIDTH)
-        hi = x.astype(BF16)
-        lo = (x - hi.astype(F32)).astype(BF16)
-        t = table[...]
-        out = jnp.dot(hi, t, preferred_element_type=F32) + jnp.dot(lo, t, preferred_element_type=F32)
-        out = (out * PLANE_SCALE).reshape(m, LOOKS, CELLS)
-        own = len(STAGES[stage])
-        for i in range(own):
-            res[c, STARTS[stage] + i] = out[i]
-            rim[0, STARTS[stage] + i], rim[1, STARTS[stage] + i] = rims(out[i])
-        places = [(own + i, (p0, p1)) for i, ((_, p0), (_, p1)) in enumerate(BACK[stage])]
-        if stage in BACK_POWER:
-            places += [(2, (p0, p1)) for p0, p1 in zip(*BACK_POWER[stage], strict=True)]
+            sums[at0 + n] = jnp.zeros((LOOKS, WIDTH), F32)
+        out = None
+        for at, width in spans:
+            x = sums[at0 : at0 + m, :, at : at + width].reshape(m * LOOKS, width)
+            hi = x.astype(BF16)
+            lo = (x - hi.astype(F32)).astype(BF16)
+            t = table[at : at + width, :]
+            y = jnp.dot(hi, t, preferred_element_type=F32) + jnp.dot(lo, t, preferred_element_type=F32)
+            out = y if out is None else out + y
+        return out
+
+    def as_planes(out):
+        return (out * PLANE_SCALE).reshape(out.shape[0] // LOOKS, LOOKS, CELLS)
+
+    def put_back(places, out):
         for i, place in places:
             place = by_core(place)
             back[place] = out[i]
             back_rim[0, place], back_rim[1, place] = rims(out[i])
+
+    def put_own(stage, out):
+        for i in range(len(STAGES[stage])):
+            res[c, STARTS[stage] + i] = out[i]
+            rim[0, STARTS[stage] + i], rim[1, STARTS[stage] + i] = rims(out[i])
+        if stage in BACK_POWER:
+            put_back([(2, both) for both in zip(*BACK_POWER[stage], strict=True)], out)
+
+    def put_far(stage, out):
+        put_back([(i, (p0, p1)) for i, ((_, p0), (_, p1)) in enumerate(BACK[stage])], out)
+
+    def compute(stage):
+        out = as_planes(looked(planes_of(stage, True, True), 0, None))
+        put_own(stage, out)
+        put_far(stage, out[len(STAGES[stage]) :])
 
     def span_of(stage, core):
         if stage == 0:
@@ -342,7 +424,7 @@
             src_ref=rim.at[side, span],
             dst_ref=edge.at[side, c, span],
             send_sem=hs.at[stage, core, side],
-            recv_sem=hr.at[stage, c, side],
+            recv_sem=hr.at[stage],
             device_id=device(0, core, ds),
             device_id_type=MESH,
         )
@@ -359,12 +441,12 @@
             src_ref=src,
             dst_ref=dst,
             send_sem=bs.at[m, 1 + ds],
-            recv_sem=br.at[m, 1 + ds],
+            recv_sem=br.at[m, 0 if ds == 0 else 1],
             device_id=device(-1, core, ds),
             device_id_type=MESH,
         )
 
-    def all_sends(stage, act):
+    def back_sends(stage, act):
         for here in range(2):
             specs = [m for m, spec in enumerate(BACK_SENDS) if spec[0] == stage and spec[1] == here]
             if specs:
@@ -378,6 +460,7 @@
                             for m in specs:
                                 act(back_send(m, ds))
 
+    def own_sends(stage, act):
         for ds in (-1, 1):
 
             @when(side_ok(ds))
@@ -387,59 +470,38 @@
 
         act(core_send(stage))
 
+    def all_sends(stage, act):
+        back_sends(stage, act)
+        own_sends(stage, act)
+
+    def wait_for(ref, sem):
+        pltpu.make_async_copy(ref, ref, sem).wait()
+
+    def edge_wait(h, span, sem):
+        here = edge if h is None else edge.at[:, pl.ds(h, 1)]
+        when(has_up, has_down)(lambda: wait_for(here.at[:, :, span], sem))
+        when(jnp.logical_not(has_up))(lambda: wait_for(here.at[1, :, span], sem))
+        when(jnp.logical_not(has_down))(lambda: wait_for(here.at[0, :, span], sem))
+
     def own_arrivals(stage):
-        ref = res.at[other, span_of(stage, c)]
-        pltpu.make_async_copy(ref, ref, pr.at[stage]).wait()
-        for ds in (-1, 1):
-            side = (1 - ds) // 2
+        wait_for(res.at[other, span_of(stage, c)], pr.at[stage])
+        if stage == 0:
             for core in range(2):
-                first_, size = NEEDS[stage][core]
-
-                @when(side_ok(-ds), c == core)
-                def _():
-                    for h in range(2):
-                        ref = edge.at[side, h, pl.ds(STARTS[stage] + first_, size)]
-                        pltpu.make_async_copy(ref, ref, hr.at[stage, h, side]).wait()
+                first_, size = NEEDS[0][core]
+                pl.when(c == core)(lambda: edge_wait(None, pl.ds(first_, size), hr.at[0]))
+        else:
+            edge_wait(None, span_of(stage, c), hr.at[stage])
 
     def back_arrivals(stage):
         for core in range(2):
-            for ds in (0, -1, 1):
-
-                @when(has_next, c == core, side_ok(-ds))
-                def _():
-                    for m, (after, h, to, first_, size) in enumerate(BACK_SENDS):
-                        if after == stage and to == core:
-                            span = pl.ds(N_OWN + first_, size)
-                            ref = res.at[h, span] if ds == 0 else edge.at[(1 - ds) // 2, h, span]
-                            pltpu.make_async_copy(ref, ref, br.at[m, 1 + ds]).wait()
-
-    own_copy.wait()
-    second_copy.wait()
-    count_copy.wait()
-    swap.wait_recv()
-    for a in range(4):
-        reorder(0, a)
-    compute(0)
-    all_sends(0, start)
-    swap.wait_send()
-    for stage in range(1, 5):
-        b, a = by_core(NEXT[stage - 1]), by_core(PREV[stage - 1])
-        wait_tile(1, b)
-        reorder(1, b)
-        wait_tile(-1, a)
-        reorder(-1, a)
-        compute(stage)
-        all_sends(stage, start)
-        if stage <= 2:
-            pass_on(stage - 1)
-        all_sends(stage - 1, wait_send)
-        own_arrivals(stage - 1)
-    tile_sends(wait_send)
-    for step in range(2):
-        passed_on(step)
-    back_arrivals(3)
-    own_arrivals(4)
-    back_arrivals(4)
+
+            @when(has_next, c == core)
+            def _():
+                for m, (after, h, to, first_, size) in enumerate(BACK_SENDS):
+                    if after == stage and to == core:
+                        span = pl.ds(N_OWN + first_, size)
+                        wait_for(res.at[h, span], br.at[m, 0])
+                        edge_wait(h, span, br.at[m, 1])
 
     def low(p0, p1):
         return jnp.where(left, p0, pltpu.roll(p1, CELLS // 2, 1))
@@ -462,48 +524,87 @@
             total = total + jnp.where(lane8 < CELLS - k, pltpu.roll(x, CELLS - k, 1), 0.0)
         return total
 
-    def table_of(a, b, entries):
-        value = 0
-        for (ea, eb), place in entries.items():
-            value = jnp.where(jnp.logical_and(a == ea, b == eb), place, value)
-        return value
+    def ref_boxes():
+        for j in range(2):
+            r0, r1 = rows_box(0, 5 + j), rows_box(1, 5 + j)
+            box_ref[j] = cells_box(jnp.where(c == 0, low(r0, r1), high(r0, r1)))
+
+    def coherences(step):
+        for core in range(2):
+
+            @pl.when(c == core)
+            def _():
+                for j, off, place, sec, half in finals(core, step):
+                    p0, p1 = res[0, place[0]], res[1, place[1]]
+                    every_ifg[j, off - 1, 0] = low(p0, p1)
+                    every_ifg[j, off - 1, 1] = high(p0, p1)
+                    b0, b1 = rows_box(0, place[0]), rows_box(1, place[1])
+                    s0, s1 = rows_box(0, sec[0]), rows_box(1, sec[1])
+                    box_r, box_i = cells_box(low(b0, b1)), cells_box(high(b0, b1))
+                    box_s = cells_box(high(s0, s1) if half else low(s0, s1))
+                    top = jnp.sqrt(box_r * box_r + box_i * box_i)
+                    every_coh[j, off - 1] = top / jnp.sqrt(box_ref[j] * box_s)
+
+    own_copy.wait()
+    second_copy.wait()
+    count_copy.wait()
+    chosen = []
+    for j in range(2):
+        for slot in range(SLOTS):
+            off = jnp.clip(second[j, slot] - (4 * q + 2 * c + j), 1, OFFS)
+            chosen.append((j, slot, off - 1, slot < count[j]))
+    swap.wait_recv()
+    for a in range(4):
+        reorder(0, a, None)
+    compute(0)
+    all_sends(0, start)
+    swap.wait_send()
+    for stage in range(1, 5):
+        b, a = by_core(NEXT[stage - 1]), by_core(PREV[stage - 1])
+        if stage < 4:
+            get_tile(1, b, None)
+            get_tile(-1, a, None)
+            compute(stage)
+            all_sends(stage, start)
+        else:
+            own, far = planes_of(4, True, False), planes_of(4, False, True)
+            get_tile(1, b, 0)
+            own_out = looked(own, 0, 0)
+            get_tile(-1, a, 0)
+            far_out = looked(far, 6, 0)
+            get_tile(1, b, 1)
+            put_own(4, as_planes(own_out + looked(own, 0, 1)))
+            own_sends(4, start)
+            get_tile(-1, a, 1)
+            put_far(4, as_planes(far_out + looked(far, 6, 1)))
+            back_sends(4, start)
+        if stage == 1:
+            pass_on(0)
+        if stage == 2:
+            pass_on(1)
+            pass_on(2)
+        all_sends(stage - 1, wait_send)
+        own_arrivals(stage - 1)
+        if stage == 1:
+            ref_boxes()
+            coherences(0)
+        if stage == 3:
+            coherences(1)
+    tile_sends(wait_send)
+    for n in range(3):
+        passed_on(n)
+    own_arrivals(4)
+    coherences(2)
+    back_arrivals(3)
+    coherences(3)
+    back_arrivals(4)
+    coherences(4)
 
     zero = jnp.zeros((LOOKS, CELLS), F32)
-    for j in range(2):
-        a = 2 * c + j
-        p = 5 + j
-        r0, r1 = rows_box(0, p), rows_box(1, p)
-        box_ref = cells_box(jnp.where(c == 0, low(r0, r1), high(r0, r1)))
-        for s in range(SLOTS):
-            used = s < count[j]
-            off = jnp.clip(second[j, s] - (4 * q + a), 1, OFFS)
-            near, middle = off <= 3 - a, off <= 7 - a
-            e = lax.rem(a + off, 4)
-            same = off - 1 + jnp.where(a == 0, 0, jnp.where(a == 1, 3, 7))
-            planes, secs = [], []
-            for h in range(2):
-                here = e if h == 0 else jnp.where(e >= 2, e - 2, e + 2)
-                step = jnp.where(here == 1, 2, jnp.where(here == 2, 1, here))
-                up = jnp.where(jnp.logical_and(lax.rem(step, 2) == 1, a >= 2), 1, 0)
-                following = 8 + 4 * step + jnp.where(step >= 2, 1, 0) + a + up
-                far = N_OWN + table_of(a, e, FAR[h])
-                planes.append(jnp.where(near, same, jnp.where(middle, following, far)))
-                power2 = BACK_POWER[2][h]
-                power4 = BACK_POWER[4][h]
-                far_even = N_OWN + jnp.where(c == 0, power2[0], power2[1])
-                far_odd = N_OWN + jnp.where(c == 0, power4[0], power4[1])
-                sec_even = jnp.where(near, 5, jnp.where(middle, 14, far_even))
-                sec_odd = jnp.where(near, 6, jnp.where(middle, 23, far_odd))
-                secs.append(jnp.where(lax.rem(e, 2) == 1, sec_odd, sec_even))
-            p0, p1 = res[0, planes[0]], res[1, planes[1]]
-            ifg[j, s, 0] = jnp.where(used, low(p0, p1), zero)
-            ifg[j, s, 1] = jnp.where(used, high(p0, p1), zero)
-            b0, b1 = rows_box(0, planes[0]), rows_box(1, planes[1])
-            s0, s1 = rows_box(0, secs[0]), rows_box(1, secs[1])
-            box_r, box_i = cells_box(low(b0, b1)), cells_box(high(b0, b1))
-            box_s = cells_box(jnp.where(e >= 2, high(s0, s1), low(s0, s1)))
-            value = jnp.sqrt(box_r * box_r + box_i * box_i) / jnp.sqrt(box_ref * box_s)
-            coh[j, s] = jnp.where(used, value, zero)
+    for j, slot, off, used in chosen:
+        for part in range(2):
+            ifg[j, slot, part] = jnp.where(used, every_ifg[j, off, part], zero)
+        coh[j, slot] = jnp.where(used, every_coh[j, off], zero)
 
     all_sends(4, wait_send)
 
@@ -543,6 +644,9 @@
             pltpu.VMEM((2, N_BACK, 4, CELLS), F32),
             pltpu.SMEM((2, SLOTS), jnp.int32),
             pltpu.SMEM((2,), jnp.int32),
+            pltpu.VMEM((2, OFFS, 2, LOOKS, CELLS), F32),
+            pltpu.VMEM((2, OFFS, LOOKS, CELLS), F32),
+            pltpu.VMEM((2, LOOKS, CELLS), F32),
             dma,
             dma((2,)),
             dma,
@@ -551,13 +655,17 @@
             dma((4,)),
             dma((2, 2)),
             dma((4,)),
-            dma((2,)),
+            dma,
+            dma((4,)),
+            dma,
+            dma((4,)),
+            dma((3,)),
             dma((5,)),
             dma((5,)),
             dma((5, 2, 2)),
-            dma((5, 2, 2)),
+            dma((5,)),
             dma((8, 3)),
-            dma((8, 3)),
+            dma((8, 2)),
         ],
         compiler_params=pltpu.CompilerParams(
             collective_id=0, has_side_effects=True, vmem_limit_bytes=40 * 2**20

time: 37 us -> 34.5 us (0.932)
  Pallas kernels: 36.3 us -> 33.8 us
    pallas_call x1, Pallas kernels: 35.6 us -> 33.1 us  [shards(): pl.pallas_call(planes_kernel, out_shape=(pltpu.VMEM(ifg_shape, F32), pltp...]
where the time goes in v3:
time: 34.5 us
  Pallas kernels  33.8 us (98%)
  between operations  0.64 us (2%)
    pallas_call x1, Pallas kernels, shards(): pl.pallas_call(planes_kernel, out_shape=(pltpu.VMEM(ifg_shape, F32), pltp...  33.1 us

profile of v3, /device:TPU:25, one launch (start us, length us, event | category | flops | bytes accessed | tf_op | source)
XLA Modules:
  0.0 34.5 jit_solution(17921466961356047950)
XLA Ops:
  0.6 33.1 %shard_map.50 = (f32[2,6,2,8,128]{4,3,2,1,0:T(8,128)S(1)}, f32[2,6,8,128]{3,2,1,0:T(8,128)S(1)}) custom-call(bf16[2,2,40,2560]{3,2,1,0:T(8,128)(2,1)} %slc.1, s32[2,6]{1,0:T(2,128)} %second_in.1, s32[2]{0:T(128)} %count_in.1), custom_call_target="tpu_custom_call" | custom-call | tf_op jit(solution)/shard_map/pallas_call | solution.py:630
  33.8 0.7 %shard_map.51 = (f32[2,6,2,8,128]{4,3,2,1,0:T(8,128)}, f32[2,6,8,128]{3,2,1,0:T(8,128)}) custom-call(f32[2,6,2,8,128]{4,3,2,1,0:T(8,128)S(1)} %get-tuple-element.4.ifg, f32[2,6,8,128]{3,2,1,0:T(8,128)S(1)} %get-tuple-element.5.coh), custom_call_target="tpu_custom_call" | custom-call | tf_op jit(solution)/shard_map/pallas_call | solution.py:674

commit v4 on v3

--- a/solution.py
+++ b/solution.py
@@ -118,7 +118,7 @@
 
 def planes_kernel(
     slc, second_in, count_in, ifg, coh, res, edge, tiles, looks, sums, table, back, rim, back_rim, second, count, every_ifg, every_coh, box_ref,
-    lsem, sem2, xs, xr, us, ur, vs, vr, us2, ur2, vs2, vr2, fs, ps, pr, hs, hr, bs, br,
+    ready, lsem, sem2, xs, xr, us, ur, vs, vr, us2, ur2, vs2, vr2, fs, ps, pr, hs, hr, bs, br,
 ):
     date = lax.axis_index("date")
     strip = lax.axis_index("strip")
@@ -142,6 +142,28 @@
             return jnp.where(c == 0, x[0], x[1])
         return x
 
+    barrier = pltpu.get_barrier_semaphore()
+    last, mid = CHIPS - 1, CHIPS // 2
+
+    def hello(semaphore, chip, core, row):
+        pl.semaphore_signal(semaphore, inc=1, device_id=(chip * 2 + core, row), device_id_type=MESH)
+
+    def hello_both(semaphore, chip):
+        for core in range(2):
+            hello(semaphore, chip, core, strip)
+
+    pl.when(q == 0)(lambda: hello_both(barrier, mid))
+    pl.when(q == mid - 1)(lambda: hello_both(barrier, last))
+
+    def waits_apart(chip):
+        return jnp.logical_and(chip % 8 >= 3, chip % 8 <= 3)
+
+    when(has_prev, jnp.logical_not(waits_apart(q - 1)))(lambda: hello_both(barrier, q - 1))
+    when(has_next)(lambda: hello_both(barrier, q + 1))
+    when(has_up)(lambda: hello(barrier, q, c, strip - 1))
+    when(has_down)(lambda: hello(barrier, q, c, strip + 1))
+    hello(barrier, q, other, strip)
+
     own_copy = pltpu.make_async_copy(
         slc.at[:, :, :, pl.ds(pl.multiple_of(c * HALF, HALF), HALF)], tiles.at[1, pl.ds(2 * c, 2)], lsem
     )
@@ -151,39 +173,14 @@
     second_copy.start()
     count_copy.start()
 
-    barrier = pltpu.get_barrier_semaphore()
-    for dq in (-1, 1):
-
-        @when(chip_ok(dq))
-        def _():
-            for core in range(2):
-                pl.semaphore_signal(barrier, inc=1, device_id=device(dq, core, 0), device_id_type=MESH)
-
-    pl.semaphore_signal(barrier, inc=1, device_id=device(0, other, 0), device_id_type=MESH)
-    for ds in (-1, 1):
-
-        @when(side_ok(ds))
-        def _():
-            pl.semaphore_signal(barrier, inc=1, device_id=device(0, c, ds), device_id_type=MESH)
-
-    last, mid = CHIPS - 1, CHIPS // 2
-
-    def hello(chip, cores):
-        for core in cores:
-            pl.semaphore_signal(barrier, inc=1, device_id=(chip * 2 + core, strip), device_id_type=MESH)
-
-    pl.when(q == 0)(lambda: hello(mid, (0, 1)))
-    pl.when(q == mid - 1)(lambda: hello(0, (c,)))
-    pl.when(q == last)(lambda: hello(mid - 1, (0, 1)))
-    pl.when(q == mid)(lambda: hello(last, (c,)))
-
     def as_int(x):
         return jnp.where(x, 1, 0)
 
-    relays = jnp.logical_or(q == 0, q == last)
-    relayed = jnp.logical_or(q == mid - 1, q == mid)
-    greeted = 1 + 2 * (as_int(has_prev) + as_int(has_next)) + as_int(has_up) + as_int(has_down)
-    pl.semaphore_wait(barrier, greeted + as_int(relays) + 2 * as_int(relayed))
+    apart = jnp.logical_and(has_next, waits_apart(q))
+    greeted = 1 + 2 * (as_int(has_prev) + as_int(has_next) - as_int(apart)) + as_int(has_up) + as_int(has_down)
+    pl.semaphore_wait(barrier, greeted + 2 * as_int(jnp.logical_or(q == mid, q == last)))
+    when(has_prev, waits_apart(q - 1))(lambda: hello_both(ready, q - 1))
+    pl.when(q == last)(lambda: hello_both(ready, mid - 1))
 
     swap = pltpu.make_async_remote_copy(
         src_ref=slc.at[:, :, :, pl.ds(pl.multiple_of(other * HALF, HALF), HALF)],
@@ -193,6 +190,8 @@
         device_id=device(0, other, 0),
         device_id_type=MESH,
     )
+
+    PASSED = {-1: [(2, None), (3, 0), (3, 1)], 1: [(2, None)]}
 
     def tile_copy(dq, j, core, relay, part):
         send, recv = (us.at[j, core], ur) if dq < 0 else (vs.at[j, core], vr)
@@ -215,15 +214,14 @@
             device_id_type=MESH,
         )
 
-    PARTS = [(0, None), (1, 0), (1, 1)]
-
     def part_of(ref, part):
         if part is None:
             return ref
         return ref.at[:, :, pl.ds(part * HALF // 2, HALF // 2)]
 
     def forward_copy(n, at_first):
-        step, part = PARTS[n]
+        which, part = PASSED[-1 if at_first else 1][n]
+        step = which - 2
         a = by_core((NEXT if at_first else PREV)[2 + step])
         side = 2 if at_first else 0
         came, recv = (vr, ur) if at_first else (ur, vr)
@@ -246,14 +244,18 @@
             pltpu.make_async_copy(here, here, came).wait()
             copy.start()
 
-        pl.when(q == 0)(lambda: one(True))
-        pl.when(q == last)(lambda: one(False))
+        if n < len(PASSED[-1]):
+            pl.when(q == 0)(lambda: one(True))
+        if n < len(PASSED[1]):
+            pl.when(q == last)(lambda: one(False))
 
     def passed_on(n):
-        pl.when(q == 0)(lambda: forward_copy(n, True)[2].wait_send())
-        pl.when(q == last)(lambda: forward_copy(n, False)[2].wait_send())
-
-    def tile_sends(act):
+        if n < len(PASSED[-1]):
+            pl.when(q == 0)(lambda: forward_copy(n, True)[2].wait_send())
+        if n < len(PASSED[1]):
+            pl.when(q == last)(lambda: forward_copy(n, False)[2].wait_send())
+
+    def tile_sends(act, times=(0, 1)):
         for here in range(2):
 
             @pl.when(c == here)
@@ -267,13 +269,19 @@
 
                         def send_parts(relay):
                             for part in (0, 1) if n == 3 else (None,):
-                                act(tile_copy(dq, j, core, relay, part))
-
-                        if n < 2:
-                            when(chip_ok(dq))(lambda: send_parts(False))
-                        else:
-                            when(chip_ok(dq), jnp.logical_not(far))(lambda: send_parts(False))
-                            when(far)(lambda: send_parts(True))
+                                if relay is None or relay == ((n, part) in PASSED[dq]):
+                                    act(tile_copy(dq, j, core, bool(relay), part))
+
+                        for time in times:
+                            if dq < 0:
+                                if time == 0:
+                                    when(has_prev, jnp.logical_not(far))(lambda: send_parts(None))
+                                    when(far)(lambda: send_parts(False))
+                                    when(far)(lambda: send_parts(True))
+                            else:
+                                waiting = apart if time == 1 else jnp.logical_not(apart)
+                                when(has_next, waiting, jnp.logical_not(far))(lambda: send_parts(None))
+                                when(far)(lambda: send_parts(time == 1))
 
     def start(copy):
         copy.start()
@@ -281,8 +289,8 @@
     def wait_send(copy):
         copy.wait_send()
 
+    tile_sends(start, (0,))
     swap.start()
-    tile_sends(start)
 
     first = lax.broadcasted_iota(jnp.int32, (CELLS, CELLS), 1) * LOOK_RG
     lane = lax.broadcasted_iota(jnp.int32, (CELLS, CELLS), 0)
@@ -294,6 +302,12 @@
         return carry
 
     lax.fori_loop(0, WIDTH // CELLS, fill, 0)
+
+    @pl.when(jnp.logical_or(apart, q == mid - 1))
+    def _():
+        pl.semaphore_wait(ready, 2)
+        tile_sends(start, (1,))
+
     row = lax.broadcasted_iota(jnp.int32, (ROWS, ROWS), 0)
     col = lax.broadcasted_iota(jnp.int32, (ROWS, ROWS), 1)
     order = jnp.where(col == LOOK_AZ * (row % LOOKS) + row // LOOKS, 1.0, 0.0).astype(BF16)
@@ -647,6 +661,7 @@
             pltpu.VMEM((2, OFFS, 2, LOOKS, CELLS), F32),
             pltpu.VMEM((2, OFFS, LOOKS, CELLS), F32),
             pltpu.VMEM((2, LOOKS, CELLS), F32),
+            pltpu.SemaphoreType.REGULAR,
             dma,
             dma((2,)),
             dma,

time: 34.5 us -> 33.3 us (0.965); the launches traced: 34.5 us -> 32.7 us
  Pallas kernels: 33.8 us -> 32.1 us
    pallas_call x1, Pallas kernels: 33.1 us -> 31.4 us  [shards(): pl.pallas_call(planes_kernel, out_shape=(pltpu.VMEM(ifg_shape, F32), pltp...]
where the time goes in v4:
time: 33.3 us; the launch traced here: 32.7 us
  Pallas kernels  32.1 us (96%)
  between operations  0.64 us (2%)
    pallas_call x1, Pallas kernels, shards(): pl.pallas_call(planes_kernel, out_shape=(pltpu.VMEM(ifg_shape, F32), pltp...  31.4 us
    pallas_call x1, Pallas kernels, shards(): pl.pallas_call(store_kernel, out_shape=(jax.ShapeDtypeStruct(ifg_shape, F...  0.67 us

profile of v4, /device:TPU:25, one launch (start us, length us, event | category | flops | bytes accessed | tf_op | source)
XLA Modules:
  0.0 32.7 jit_solution(4812149097983430013)
XLA Ops:
  0.6 31.4 %shard_map.50 = (f32[2,6,2,8,128]{4,3,2,1,0:T(8,128)S(1)}, f32[2,6,8,128]{3,2,1,0:T(8,128)S(1)}) custom-call(bf16[2,2,40,2560]{3,2,1,0:T(8,128)(2,1)} %slc.1, s32[2,6]{1,0:T(2,128)} %second_in.1, s32[2]{0:T(128)} %count_in.1), custom_call_target="tpu_custom_call" | custom-call | tf_op jit(solution)/shard_map/pallas_call | solution.py:644
  32.0 0.7 %shard_map.51 = (f32[2,6,2,8,128]{4,3,2,1,0:T(8,128)}, f32[2,6,8,128]{3,2,1,0:T(8,128)}) custom-call(f32[2,6,2,8,128]{4,3,2,1,0:T(8,128)S(1)} %get-tuple-element.4.ifg, f32[2,6,8,128]{3,2,1,0:T(8,128)S(1)} %get-tuple-element.5.coh), custom_call_target="tpu_custom_call" | custom-call | tf_op jit(solution)/shard_map/pallas_call | solution.py:689

commit v5 on v4

--- a/solution.py
+++ b/solution.py
@@ -159,7 +159,7 @@
         return jnp.logical_and(chip % 8 >= 3, chip % 8 <= 3)
 
     when(has_prev, jnp.logical_not(waits_apart(q - 1)))(lambda: hello_both(barrier, q - 1))
-    when(has_next)(lambda: hello_both(barrier, q + 1))
+    when(has_next, q != mid - 1)(lambda: hello_both(barrier, q + 1))
     when(has_up)(lambda: hello(barrier, q, c, strip - 1))
     when(has_down)(lambda: hello(barrier, q, c, strip + 1))
     hello(barrier, q, other, strip)
@@ -177,10 +177,11 @@
         return jnp.where(x, 1, 0)
 
     apart = jnp.logical_and(has_next, waits_apart(q))
-    greeted = 1 + 2 * (as_int(has_prev) + as_int(has_next) - as_int(apart)) + as_int(has_up) + as_int(has_down)
+    greeted = 1 + 2 * (as_int(has_prev) + as_int(has_next) - as_int(apart) - as_int(q == mid)) + as_int(has_up) + as_int(has_down)
     pl.semaphore_wait(barrier, greeted + 2 * as_int(jnp.logical_or(q == mid, q == last)))
     when(has_prev, waits_apart(q - 1))(lambda: hello_both(ready, q - 1))
     pl.when(q == last)(lambda: hello_both(ready, mid - 1))
+    pl.when(q == mid - 1)(lambda: hello_both(ready, mid))
 
     swap = pltpu.make_async_remote_copy(
         src_ref=slc.at[:, :, :, pl.ds(pl.multiple_of(other * HALF, HALF), HALF)],
@@ -191,7 +192,7 @@
         device_id_type=MESH,
     )
 
-    PASSED = {-1: [(2, None), (3, 0), (3, 1)], 1: [(2, None)]}
+    PASSED = {-1: [(2, None), (3, 1)], 1: [(2, None)]}
 
     def tile_copy(dq, j, core, relay, part):
         send, recv = (us.at[j, core], ur) if dq < 0 else (vs.at[j, core], vr)
@@ -276,6 +277,7 @@
                             if dq < 0:
                                 if time == 0:
                                     when(has_prev, jnp.logical_not(far))(lambda: send_parts(None))
+                                else:
                                     when(far)(lambda: send_parts(False))
                                     when(far)(lambda: send_parts(True))
                             else:
@@ -303,7 +305,7 @@
 
     lax.fori_loop(0, WIDTH // CELLS, fill, 0)
 
-    @pl.when(jnp.logical_or(apart, q == mid - 1))
+    @pl.when(jnp.logical_or(apart, jnp.logical_or(q == mid - 1, q == mid)))
     def _():
         pl.semaphore_wait(ready, 2)
         tile_sends(start, (1,))
@@ -607,10 +609,10 @@
     tile_sends(wait_send)
     for n in range(3):
         passed_on(n)
+    back_arrivals(3)
+    coherences(3)
     own_arrivals(4)
     coherences(2)
-    back_arrivals(3)
-    coherences(3)
     back_arrivals(4)
     coherences(4)
 

time: 33.3 us -> 32.5 us (0.976)
  the two profiles are of different devices: /device:TPU:25 before, /device:TPU:103 now
where the time goes in v5:
time: 32.5 us; the launch traced here: 32.4 us
  Pallas kernels  31.8 us (98%)
  between operations  0.64 us (2%)
    pallas_call x1, Pallas kernels, shards(): pl.pallas_call(planes_kernel, out_shape=(pltpu.VMEM(ifg_shape, F32), pltp...  31.1 us
    pallas_call x1, Pallas kernels, shards(): pl.pallas_call(store_kernel, out_shape=(jax.ShapeDtypeStruct(ifg_shape, F...  0.67 us

profile of v5, /device:TPU:103, one launch (start us, length us, event | category | flops | bytes accessed | tf_op | source)
XLA Modules:
  0.0 32.4 jit_solution(16676724939951354195)
XLA Ops:
  0.6 31.1 %shard_map.50 = (f32[2,6,2,8,128]{4,3,2,1,0:T(8,128)S(1)}, f32[2,6,8,128]{3,2,1,0:T(8,128)S(1)}) custom-call(bf16[2,2,40,2560]{3,2,1,0:T(8,128)(2,1)} %slc.1, s32[2,6]{1,0:T(2,128)} %second_in.1, s32[2]{0:T(128)} %count_in.1), custom_call_target="tpu_custom_call" | custom-call | tf_op jit(solution)/shard_map/pallas_call | solution.py:646
  31.7 0.7 %shard_map.51 = (f32[2,6,2,8,128]{4,3,2,1,0:T(8,128)}, f32[2,6,8,128]{3,2,1,0:T(8,128)}) custom-call(f32[2,6,2,8,128]{4,3,2,1,0:T(8,128)S(1)} %get-tuple-element.4.ifg, f32[2,6,8,128]{3,2,1,0:T(8,128)S(1)} %get-tuple-element.5.coh), custom_call_target="tpu_custom_call" | custom-call | tf_op jit(solution)/shard_map/pallas_call | solution.py:691

commit v6 on v5

--- a/solution.py
+++ b/solution.py
@@ -389,7 +389,8 @@
             hi = x.astype(BF16)
             lo = (x - hi.astype(F32)).astype(BF16)
             t = table[at : at + width, :]
-            y = jnp.dot(hi, t, preferred_element_type=F32) + jnp.dot(lo, t, preferred_element_type=F32)
+            both = jnp.dot(jnp.concatenate([hi, lo], axis=0), t, preferred_element_type=F32)
+            y = both[0 : m * LOOKS] + both[m * LOOKS :]
             out = y if out is None else out + y
         return out
 
@@ -613,6 +614,7 @@
     coherences(3)
     own_arrivals(4)
     coherences(2)
+    all_sends(4, wait_send)
     back_arrivals(4)
     coherences(4)
 
@@ -621,8 +623,6 @@
         for part in range(2):
             ifg[j, slot, part] = jnp.where(used, every_ifg[j, off, part], zero)
         coh[j, slot] = jnp.where(used, every_coh[j, off], zero)
-
-    all_sends(4, wait_send)
 
 
 def store_kernel(ifg, coh, ifg_out, coh_out, sems):

time: 32.5 us -> 32.5 us (level)
  the two profiles are of different devices: /device:TPU:103 before, /device:TPU:119 now
where the time goes in v6:
time: 32.5 us; the launch traced here: 32.4 us
  Pallas kernels  31.7 us (98%)
  between operations  0.64 us (2%)
    pallas_call x1, Pallas kernels, shards(): pl.pallas_call(planes_kernel, out_shape=(pltpu.VMEM(ifg_shape, F32), pltp...  31 us
    pallas_call x1, Pallas kernels, shards(): pl.pallas_call(store_kernel, out_shape=(jax.ShapeDtypeStruct(ifg_shape, F...  0.67 us

profile of v6, /device:TPU:119, one launch (start us, length us, event | category | flops | bytes accessed | tf_op | source)
XLA Modules:
  0.0 32.4 jit_solution(11412935177462298987)
XLA Ops:
  0.6 31.0 %shard_map.50 = (f32[2,6,2,8,128]{4,3,2,1,0:T(8,128)S(1)}, f32[2,6,8,128]{3,2,1,0:T(8,128)S(1)}) custom-call(bf16[2,2,40,2560]{3,2,1,0:T(8,128)(2,1)} %slc.1, s32[2,6]{1,0:T(2,128)} %second_in.1, s32[2]{0:T(128)} %count_in.1), custom_call_target="tpu_custom_call" | custom-call | tf_op jit(solution)/shard_map/pallas_call | solution.py:646
  31.7 0.7 %shard_map.51 = (f32[2,6,2,8,128]{4,3,2,1,0:T(8,128)}, f32[2,6,8,128]{3,2,1,0:T(8,128)}) custom-call(f32[2,6,2,8,128]{4,3,2,1,0:T(8,128)S(1)} %get-tuple-element.4.ifg, f32[2,6,8,128]{3,2,1,0:T(8,128)S(1)} %get-tuple-element.5.coh), custom_call_target="tpu_custom_call" | custom-call | tf_op jit(solution)/shard_map/pallas_call | solution.py:691

commit v7 on v6

--- a/solution.py
+++ b/solution.py
@@ -152,6 +152,8 @@
         for core in range(2):
             hello(semaphore, chip, core, strip)
 
+    when(has_up)(lambda: hello(barrier, q, c, strip - 1))
+    when(has_down)(lambda: hello(barrier, q, c, strip + 1))
     pl.when(q == 0)(lambda: hello_both(barrier, mid))
     pl.when(q == mid - 1)(lambda: hello_both(barrier, last))
 
@@ -160,8 +162,6 @@
 
     when(has_prev, jnp.logical_not(waits_apart(q - 1)))(lambda: hello_both(barrier, q - 1))
     when(has_next, q != mid - 1)(lambda: hello_both(barrier, q + 1))
-    when(has_up)(lambda: hello(barrier, q, c, strip - 1))
-    when(has_down)(lambda: hello(barrier, q, c, strip + 1))
     hello(barrier, q, other, strip)
 
     own_copy = pltpu.make_async_copy(

time: 32.5 us -> 32.4 us (level)
  the two profiles are of different devices: /device:TPU:119 before, /device:TPU:101 now
where the time goes in v7:
time: 32.4 us; the launch traced here: 32.3 us
  Pallas kernels  31.7 us (98%)
  between operations  0.64 us (2%)
    pallas_call x1, Pallas kernels, shards(): pl.pallas_call(planes_kernel, out_shape=(pltpu.VMEM(ifg_shape, F32), pltp...  31 us
    pallas_call x1, Pallas kernels, shards(): pl.pallas_call(store_kernel, out_shape=(jax.ShapeDtypeStruct(ifg_shape, F...  0.67 us

profile of v7, /device:TPU:101, one launch (start us, length us, event | category | flops | bytes accessed | tf_op | source)
XLA Modules:
  0.0 32.3 jit_solution(6931945099067194447)
XLA Ops:
  0.6 31.0 %shard_map.50 = (f32[2,6,2,8,128]{4,3,2,1,0:T(8,128)S(1)}, f32[2,6,8,128]{3,2,1,0:T(8,128)S(1)}) custom-call(bf16[2,2,40,2560]{3,2,1,0:T(8,128)(2,1)} %slc.1, s32[2,6]{1,0:T(2,128)} %second_in.1, s32[2]{0:T(128)} %count_in.1), custom_call_target="tpu_custom_call" | custom-call | tf_op jit(solution)/shard_map/pallas_call | solution.py:646
  31.6 0.7 %shard_map.51 = (f32[2,6,2,8,128]{4,3,2,1,0:T(8,128)}, f32[2,6,8,128]{3,2,1,0:T(8,128)}) custom-call(f32[2,6,2,8,128]{4,3,2,1,0:T(8,128)S(1)} %get-tuple-element.4.ifg, f32[2,6,8,128]{3,2,1,0:T(8,128)S(1)} %get-tuple-element.5.coh), custom_call_target="tpu_custom_call" | custom-call | tf_op jit(solution)/shard_map/pallas_call | solution.py:691
